TPU v7x, 512 devices: a whole 4x8x8 slice. The times are simulated.
512 devices in a mesh: expert: 128 (over z, y, core), dp: 4 (over x).
Axes of the slice: x: 4, y: 8, z: 8, core: 2. Of those that a mesh axis runs over, the one named last changes fastest.
Arguments:
- grads: bfloat16 [4, 256, 128, 1536], P('dp', 'expert'), may hold values from -6 to 6
- master: float32 [128, 128, 1536], P('expert', 'dp'), may hold values from -0.12 to 0.12
- moment: float32 [128, 128, 1536], P('expert', 'dp'), may hold values from -0.4 to 0.4
- second: float32 [128, 128, 1536], P('expert', 'dp'), may hold values from 0.001 to 0.01
- old_place: int32 [128, 2], replicated, may hold values from 0 to 127, all different within a row
- new_place: int32 [128, 2], replicated, may hold values from 0 to 127, all different within a row
- owner_slot: int32 [128], replicated, may hold values from 0 to 127, as said below
Outputs:
- new_master: float32 [128, 128, 1536], P('expert', 'dp')
- new_moment: float32 [128, 128, 1536], P('expert', 'dp')
- new_second: float32 [128, 128, 1536], P('expert', 'dp')
- replicas: bfloat16 [256, 128, 1536], P('expert', 'dp')
Inputs may be any that keep to these rules, and one draw needn't show every extreme that they name: `owner_slot`: distinct values; the expert's owner is device value // 1 of the expert axis, in its owner slot value % 1. Slots that no expert names hold unused state. `old_place`: each device's 2 slots name distinct experts; every expert is named by some slot. `new_place`: each device's 2 slots name distinct experts; every expert is named by some slot.
All inputs are finite; a program needn't handle non-finite values.
Results may differ from a plain program's by a relative error of at most 0.015.
Values may be sent and summed in bfloat16 or wider, within the bound.
No kernel may reach another device: no remote copies, remote signals or barrier semaphores. Data moves between devices by JAX's collectives and lax.ppermute only.
A program may use at most 64 MiB of HBM per device.

v0:
```python
import jax
import jax.numpy as jnp
from jax import lax
from jax.sharding import PartitionSpec as P

beta_first = 0.9
beta_second = 0.999
learn_rate = 0.02
weight_decay = 0.1
epsilon = 1e-08
scale_first = 1.0 - 0.9**40
scale_second = 1.0 - 0.999**40


def on_device(grads, master, moment, second, old_place, new_place, owner_slot):
    device_count = lax.axis_size("expert")
    slot_count = grads.shape[1]
    col_count = grads.shape[3]
    own_count = master.shape[0]
    quarter_rows = master.shape[1]
    piece_size = quarter_rows * col_count // device_count
    expert_count = owner_slot.shape[0]
    expert_ids = jnp.arange(expert_count, dtype=jnp.int32)
    old_hot = (expert_ids[:, None] == old_place.T.reshape(-1)[None, :]).astype(jnp.float32)
    summed = lax.psum_scatter(
        grads[0].astype(jnp.float32).astype(jnp.bfloat16), "dp", scatter_dimension=1, tiled=True
    ).astype(jnp.float32)
    incoming = lax.all_to_all(
        summed.reshape(slot_count, device_count, piece_size),
        "expert",
        split_axis=1,
        concat_axis=1,
        tiled=True,
    )
    expert_part = jnp.dot(
        old_hot,
        incoming.reshape(slot_count * device_count, piece_size),
        precision=lax.Precision.HIGHEST,
    )
    slot_ids = jnp.arange(device_count * own_count, dtype=jnp.int32)
    owner_hot = (
        (slot_ids[:, None] == owner_slot[None, :])
        .astype(jnp.float32)
        .reshape(device_count, own_count, expert_count)
    )
    outgoing = jnp.einsum("koe,ep->okp", owner_hot, expert_part, precision=lax.Precision.HIGHEST)
    slot_grad = lax.all_to_all(outgoing, "expert", split_axis=1, concat_axis=1, tiled=True).reshape(
        own_count, quarter_rows, col_count
    )
    new_moment = beta_first * moment + (1.0 - beta_first) * slot_grad
    new_second = beta_second * second + (1.0 - beta_second) * slot_grad * slot_grad
    update = new_moment / scale_first / (jnp.sqrt(new_second / scale_second) + epsilon)
    new_master = master - learn_rate * (update + weight_decay * master)
    fresh = new_master.astype(jnp.bfloat16).reshape(own_count, device_count, piece_size)
    every_slot = lax.all_to_all(fresh, "expert", split_axis=1, concat_axis=0, tiled=True).reshape(
        device_count * own_count, piece_size
    )
    wanted = owner_slot[new_place.T.reshape(-1)]
    outbound = jnp.take(every_slot, wanted, axis=0).reshape(slot_count, device_count, piece_size)
    received = lax.all_to_all(outbound, "expert", split_axis=1, concat_axis=1, tiled=True)
    replicas = received.reshape(slot_count, quarter_rows, col_count)
    return (new_master, new_moment, new_second, replicas)


def solution(mesh):
    placed = (
        P("dp", "expert", None, None),
        P("expert", "dp", None),
        P("expert", "dp", None),
        P("expert", "dp", None),
        P(),
        P(),
        P(),
    )
    return jax.shard_map(
        on_device,
        mesh=mesh,
        in_specs=placed,
        out_specs=(
            P("expert", "dp", None),
            P("expert", "dp", None),
            P("expert", "dp", None),
            P("expert", "dp", None),
        ),
        check_vma=False,
    )
```

profile of v0, /device:TPU:1, one launch (start us, length us, event | category | flops | bytes accessed | tf_op | source)
XLA Modules:
  0.0 151.2 jit_solution(746440134408523592)
XLA Ops:
  7.2 0.0 reduce-scatter.2.cloned.1.call-start
  7.2 0.7 reduce-scatter.2.cloned.1.call-update
  7.9 35.2 %reduce-scatter.2.cloned.1.call-done = bf16[2,32,1536]{2,1,0:T(8,128)(2,1)} async-done(((bf16[2,128,1536]{2,1,0:T(8,128)(2,1)}), bf16[2,32,1536]{2,1,0:T(8,128)(2,1)}) %reduce-scatter.2.cloned.1.call-update) | async-done | bytes 196624 | tf_op jit(solution)/shard_map/reduce_scatter | solution.py:25
  43.0 1.0 reshape.149
  44.1 0.3 copy.15
  44.4 33.0 %all_to_all.24 = f32[2,128,384]{2,0,1:T(2,128)S(1)} all-to-all(f32[2,128,384]{2,0,1:T(2,128)S(1)} %copy.15), channel_id=1, replica_groups=mesh['expert'=128,'dp'=4] {'expert'}, dimensions={1} | all-to-all | bytes 786432 | tf_op jit(solution)/shard_map/all_to_all | solution.py:28
  77.5 0.0 copy-start.4
  77.5 0.7 copy-done.4
  78.2 0.0 copy-start
  78.2 0.3 fusion.1
  78.5 0.3 copy-done
  78.8 0.4 convolution_bitcast_fusion
  79.2 0.8 copy.17
  80.0 5.3 %all-to-all-start.1 = ((f32[1,128,384]{2,0,1:T(1,128)}), f32[1,128,384]{2,0,1:T(1,128)S(1)}, u32[]{:S(2)}, u32[]{:S(2)}) async-start(f32[1,128,384]{2,0,1:T(1,128)} %copy.17), calls=%async_computation.2 | async-start | bytes 393216 | tf_op jit(solution)/shard_map/all_to_all | solution.py:47
  85.3 0.0 copy-start.5
  85.3 0.7 copy-done.5
  86.0 1.9 %gather_fusion = s32[256]{0:T(256)S(1)} fusion(s32[128]{0:T(128)S(1)} %copy-done, s32[1024]{0:T(1024)S(1)} %pad_clamp_fusion.1), kind=kCustom, calls=%fused_computation | custom fusion | bytes 3072 | tf_op jit(solution)/shard_map/gather | solution.py:58
  87.9 11.5 %all-to-all-done.1 = f32[1,128,384]{2,0,1:T(1,128)S(1)} async-done(((f32[1,128,384]{2,0,1:T(1,128)}), f32[1,128,384]{2,0,1:T(1,128)S(1)}, u32[]{:S(2)}, u32[]{:S(2)}) %all-to-all-start.1) | async-done | bytes 196640 | tf_op jit(solution)/shard_map/all_to_all | solution.py:47
  99.4 0.0 copy-start.3
  99.4 0.5 reduce
  99.9 0.0 copy-start.1
  99.9 0.0 copy-start.2
  100.0 0.4 copy-done.3
  100.4 0.5 copy-done.1
  100.9 0.1 copy-done.2
  101.0 0.9 fusion.4
  101.9 0.5 broadcast.85
  102.4 1.2 reduce.1
  103.6 0.8 reshape.168
  104.4 5.6 %all-to-all-start.2 = ((bf16[128,2,192]{2,1,0:T(2,128)(2,1)}), bf16[128,2,192]{2,1,0:T(2,128)(2,1)S(1)}, u32[]{:S(2)}, u32[]{:S(2)}) async-start(bf16[128,2,192]{2,1,0:T(2,128)(2,1)} %reshape.168), calls=%async_computation.3 | async-start | bytes 262144 | tf_op jit(solution)/shard_map/all_to_all | solution.py:55
  110.0 0.1 copy.18
  110.2 12.7 %all-to-all-done.2 = bf16[128,2,192]{2,1,0:T(2,128)(2,1)S(1)} async-done(((bf16[128,2,192]{2,1,0:T(2,128)(2,1)}), bf16[128,2,192]{2,1,0:T(2,128)(2,1)S(1)}, u32[]{:S(2)}, u32[]{:S(2)}) %all-to-all-start.2) | async-done | bytes 98336 | tf_op jit(solution)/shard_map/all_to_all | solution.py:55
  122.8 0.2 reshape.169
  123.1 1.2 gather_fusion.1
  124.2 0.3 broadcast_select_fusion
  124.6 19.0 %all_to_all.25 = bf16[2,128,384]{2,0,1:T(2,128)(2,1)S(1)} all-to-all(bf16[2,128,384]{2,0,1:T(2,128)(2,1)S(1)} %broadcast_select_fusion), channel_id=1, replica_groups=mesh['expert'=128,'dp'=4] {'expert'}, dimensions={1} | all-to-all | bytes 393216 | tf_op jit(solution)/shard_map/all_to_all | solution.py:60
  143.6 0.8 reshape.147
  (10 shorter events, 0.2 us)
Async XLA Ops:
  7.2 35.9 %reduce-scatter.2.cloned.1.call-start = ((), (), s32[]{:S(2)}) async-start(), calls=%async_computation.5 | async-start | bytes 983040 | tf_op jit(solution)/shard_map/reduce_scatter | solution.py:25
  77.5 0.7 copy-start.4
  78.2 0.7 copy-start
  80.0 19.5 %all-to-all-start.1 = ((f32[1,128,384]{2,0,1:T(1,128)}), f32[1,128,384]{2,0,1:T(1,128)S(1)}, u32[]{:S(2)}, u32[]{:S(2)}) async-start(f32[1,128,384]{2,0,1:T(1,128)} %copy.17), calls=%async_computation.2 | async-start | bytes 393216 | tf_op jit(solution)/shard_map/all_to_all | solution.py:47
  85.3 0.7 copy-start.5
  99.4 0.9 copy-start.3
  99.9 1.0 copy-start.1
  99.9 1.0 copy-start.2
  104.4 18.4 %all-to-all-start.2 = ((bf16[128,2,192]{2,1,0:T(2,128)(2,1)}), bf16[128,2,192]{2,1,0:T(2,128)(2,1)S(1)}, u32[]{:S(2)}, u32[]{:S(2)}) async-start(bf16[128,2,192]{2,1,0:T(2,128)(2,1)} %reshape.168), calls=%async_computation.3 | async-start | bytes 262144 | tf_op jit(solution)/shard_map/all_to_all | solution.py:55
Sparse Core Ops, SparseCore 0:
  10.8 32.1 reduce-scatter.1
where the time goes:
time: 152 us; the launch traced here: 151 us
  waiting for transfers between devices  60 us (39%)
  blocking collectives  52 us (34%)
  between operations  14.2 us (9%)
  starting transfers between devices  10.9 us (7%)
  local copies, waits for them, and re-layouts  10.4 us (7%)
  other arithmetic  2.96 us (2%)
    reduce_scatter x1, waiting for transfers between devices, on_device(): lax.psum_scatter(grads[0].astype(jnp.float32).astype(jnp.bfloat16), 'dp',...  35.2 us
    all_to_all x1, blocking collectives, on_device(): lax.all_to_all(summed.reshape(slot_count, device_count, piece_size), 'exp...  33 us
    all_to_all x1, blocking collectives, on_device(): lax.all_to_all(outbound, 'expert', split_axis=1, concat_axis=1, tiled=True)  19 us
    all_to_all x1, waiting for transfers between devices, on_device(): lax.all_to_all(fresh, 'expert', split_axis=1, concat_axis=0, tiled=True)  12.7 us
    all_to_all x1, waiting for transfers between devices, on_device(): lax.all_to_all(outgoing, 'expert', split_axis=1, concat_axis=1, tiled=True)  11.5 us
    all_to_all x1, starting transfers between devices, on_device(): lax.all_to_all(fresh, 'expert', split_axis=1, concat_axis=0, tiled=True)  5.56 us
    all_to_all x1, starting transfers between devices, on_device(): lax.all_to_all(outgoing, 'expert', split_axis=1, concat_axis=1, tiled=True)  5.35 us
    unnamed x16, local copies, waits for them, and re-layouts  4.18 us
  transfers between devices with their start and end apart: 3, of which 3 were waited for; matrix products, arithmetic and copies ran while one was open for 1% of the time, Pallas kernels for 0%

commit v1 on v0

v1 whole, which is shorter than its diff:
```python
import jax
import jax.numpy as jnp
from jax import lax
from jax.experimental import pallas as pl
from jax.experimental.pallas import tpu as pltpu
from jax.sharding import PartitionSpec as P

beta_first = 0.9
beta_second = 0.999
learn_rate = 0.02
weight_decay = 0.1
epsilon = 1e-08
scale_first = 1.0 - 0.9**40
scale_second = 1.0 - 0.999**40

LANES = 128


def adamw(master, moment, second, grad):
    new_moment = beta_first * moment + (1.0 - beta_first) * grad
    new_second = beta_second * second + (1.0 - beta_second) * grad * grad
    update = new_moment / scale_first / (jnp.sqrt(new_second / scale_second) + epsilon)
    new_master = master - learn_rate * (update + weight_decay * master)
    return new_master, new_moment, new_second


def pack_kernel(grads, master, moment, second, out):
    copies, slots, rows, cols = grads.shape
    quarters = out.shape[1] // rows
    tall = cols // quarters // LANES
    arrays = []
    for slot in range(slots):
        total = grads[0, slot].astype(jnp.float32)
        for copy in range(1, copies):
            total = total + grads[copy, slot].astype(jnp.float32)
        arrays.append(total)
    arrays += [master[0], moment[0], second[0]]
    for a, whole in enumerate(arrays):
        whole = whole.astype(jnp.bfloat16)
        for q in range(quarters):
            for i in range(tall):
                at = (q * tall + i) * LANES
                out[a * tall + i, q * rows : (q + 1) * rows, :] = whole[:, at : at + LANES]
    for i in range(len(arrays) * tall, out.shape[0]):
        out[i] = jnp.zeros(out.shape[1:], out.dtype)


def update_kernel(pieces, old_place, new_place, owner_slot, out):
    slots, devices = old_place.shape
    span = out.shape[2]
    tall = span // LANES
    experts = owner_slot.shape[1]

    def hot(rows, values):
        at = lax.broadcasted_iota(jnp.int32, (rows, values.shape[1]), 0)
        return (at == values).astype(jnp.bfloat16)

    def dot(a, b, dims):
        return lax.dot_general(a, b, (dims, ((), ())), preferred_element_type=jnp.float32)

    owners = hot(devices, owner_slot[...])
    grad = [jnp.zeros((devices, LANES), jnp.float32) for _ in range(tall)]
    for slot in range(slots):
        held = hot(experts, old_place[slot : slot + 1, :])
        route = dot(owners, held, ((1,), (0,))).astype(jnp.bfloat16)
        for i in range(tall):
            grad[i] = grad[i] + dot(route, pieces[slot * tall + i], ((1,), (0,)))
    fresh = []
    for i in range(tall):
        master, moment, second = (
            pieces[(slots + a) * tall + i].astype(jnp.float32) for a in range(3)
        )
        new_master, _, _ = adamw(master, moment, second, grad[i])
        fresh.append(new_master.astype(jnp.bfloat16))
        out[slots, :, i * LANES : (i + 1) * LANES] = grad[i].astype(jnp.bfloat16)
    for slot in range(slots):
        held = hot(experts, new_place[slot : slot + 1, :])
        route = dot(owners, held, ((1,), (0,))).astype(jnp.bfloat16)
        for i in range(tall):
            out[slot, :, i * LANES : (i + 1) * LANES] = dot(route, fresh[i], ((0,), (0,))).astype(
                jnp.bfloat16
            )
    for i in range(slots + 1, out.shape[0]):
        out[i] = jnp.zeros(out.shape[1:], out.dtype)


def finish_kernel(pieces, master, moment, second, new_master, new_moment, new_second, replicas):
    slots, rows, cols = replicas.shape
    span = pieces.shape[2]
    for q in range(cols // span):
        here, there = pl.ds(q * rows, rows), pl.ds(q * span, span)
        for slot in range(slots):
            replicas[slot, :, there] = pieces[slot, here, :]
        grad = pieces[slots, here, :].astype(jnp.float32)
        a, b, c = adamw(master[0, :, there], moment[0, :, there], second[0, :, there], grad)
        new_master[0, :, there] = a
        new_moment[0, :, there] = b
        new_second[0, :, there] = c


def on_device(grads, master, moment, second, old_place, new_place, owner_slot):
    devices = lax.axis_size("expert")
    copies = lax.axis_size("dp")
    _, slots, full_rows, cols = grads.shape
    rows = full_rows // copies
    span = rows * cols // devices
    tall = span // LANES
    in_vmem = pl.BlockSpec(memory_space=pltpu.VMEM)

    by_rows = grads.reshape(slots, copies, rows, cols).transpose(1, 0, 2, 3)
    mine = lax.all_to_all(by_rows, "dp", split_axis=0, concat_axis=0, tiled=True)
    lines = -(-(slots + 3) * tall // 16) * 16
    packed = pl.pallas_call(
        pack_kernel,
        out_shape=jax.ShapeDtypeStruct((lines, devices, LANES), jnp.bfloat16),
        in_specs=[in_vmem] * 4,
        out_specs=in_vmem,
        name="pack",
    )(mine, master, moment, second)
    pieces = lax.all_to_all(packed, "expert", split_axis=1, concat_axis=1, tiled=True)
    outbound = pl.pallas_call(
        update_kernel,
        out_shape=jax.ShapeDtypeStruct((slots + 2, devices, span), jnp.bfloat16),
        in_specs=[in_vmem] * 4,
        out_specs=in_vmem,
        name="update",
    )(pieces, old_place.T, new_place.T, owner_slot[None, :])
    received = lax.all_to_all(outbound, "expert", split_axis=1, concat_axis=1, tiled=True)
    return pl.pallas_call(
        finish_kernel,
        out_shape=[jax.ShapeDtypeStruct(master.shape, jnp.float32)] * 3
        + [jax.ShapeDtypeStruct((slots, rows, cols), jnp.bfloat16)],
        in_specs=[in_vmem] * 4,
        out_specs=[in_vmem] * 4,
        name="finish",
    )(received, master, moment, second)


def solution(mesh):
    placed = (
        P("dp", "expert", None, None),
        P("expert", "dp", None),
        P("expert", "dp", None),
        P("expert", "dp", None),
        P(),
        P(),
        P(),
    )
    return jax.shard_map(
        on_device,
        mesh=mesh,
        in_specs=placed,
        out_specs=(
            P("expert", "dp", None),
            P("expert", "dp", None),
            P("expert", "dp", None),
            P("expert", "dp", None),
        ),
        check_vma=False,
    )
```

time: 152 us -> 92.1 us (0.61)
  waiting for transfers between devices: 60 us -> 0 us
  blocking collectives: 52 us -> 78.4 us
  between operations: 14.2 us -> 0.64 us
  starting transfers between devices: 10.9 us -> 0 us
  Pallas kernels: 0 us -> 7.09 us
  local copies, waits for them, and re-layouts: 10.4 us -> 5.58 us
  other arithmetic: 2.96 us -> 0 us
    reduce_scatter x1 -> x0, waiting for transfers between devices: 35.2 us -> none  [on_device(): lax.psum_scatter(grads[0].astype(jnp.float32).astype(jnp.bfloat16), 'dp',...]
    all_to_all x2 -> x0, waiting for transfers between devices: 24.2 us -> none  [the longest x1 12.7 us: on_device(): lax.all_to_all(fresh, 'expert', split_axis=1, concat_axis=0, tiled=True)]
    all_to_all x1 -> x2, blocking collectives: 33 us -> 55.3 us  [the longest x1 42.2 us: on_device(): lax.all_to_all(packed, 'expert', split_axis=1, concat_axis=1, tiled=True)]
    all_to_all x2 -> x0, starting transfers between devices: 10.9 us -> none  [the longest x1 5.56 us: on_device(): lax.all_to_all(fresh, 'expert', split_axis=1, concat_axis=0, tiled=True)]
    pallas_call x0 -> x3, Pallas kernels: none -> 7.09 us  [the longest x1 2.64 us: on_device(): pl.pallas_call(update_kernel, out_shape=jax.ShapeDtypeStruct((slots + 2,...]
    unnamed x16 -> x0, local copies, waits for them, and re-layouts: 4.18 us -> none
    all_to_all x1, blocking collectives: 19 us -> 23.1 us  [on_device(): lax.all_to_all(outbound, 'expert', split_axis=1, concat_axis=1, tiled=True)]
    gather x2 -> x0, local copies, waits for them, and re-layouts: 3.03 us -> none  [the longest x1 1.87 us: on_device(): wanted = owner_slot[new_place.T.reshape(-1)]]
  transfers between devices with their start and end apart: 3 -> 0, of which waited for: 3 -> 0; matrix products, arithmetic and copies ran while one was open for 1% -> 0% of each run, Pallas kernels for 0% -> 0%
where the time goes in v1:
time: 92.1 us; the launch traced here: 91.7 us
  blocking collectives  78.4 us (85%)
  Pallas kernels  7.09 us (8%)
  local copies, waits for them, and re-layouts  5.58 us (6%)
    all_to_all x1, blocking collectives, on_device(): lax.all_to_all(packed, 'expert', split_axis=1, concat_axis=1, tiled=True)  42.2 us
    all_to_all x1, blocking collectives, on_device(): lax.all_to_all(outbound, 'expert', split_axis=1, concat_axis=1, tiled=True)  23.1 us
    all_to_all x1, blocking collectives, on_device(): lax.all_to_all(by_rows, 'dp', split_axis=0, concat_axis=0, tiled=True)  13.1 us
    pallas_call x1, Pallas kernels, on_device(): pl.pallas_call(update_kernel, out_shape=jax.ShapeDtypeStruct((slots + 2,...  2.64 us
    pallas_call x1, Pallas kernels, on_device(): pl.pallas_call(pack_kernel, out_shape=jax.ShapeDtypeStruct((lines, device...  2.25 us
    pallas_call x1, Pallas kernels, on_device(): pl.pallas_call(finish_kernel, out_shape=[jax.ShapeDtypeStruct(master.shap...  2.2 us

profile of v1, /device:TPU:1, one launch (start us, length us, event | category | flops | bytes accessed | tf_op | source)
XLA Modules:
  0.0 91.7 jit_solution(10204086238506177765)
XLA Ops:
  0.6 1.2 %copy.18 = bf16[2,4,32,1536]{3,2,0,1:T(8,128)(2,1)S(1)} copy(bf16[2,4,32,1536]{3,2,1,0:T(8,128)(2,1)} %bitcast.8) | data formatting | bytes 1572864 | tf_op jit(solution)/shard_map/reshape | solution.py:110
  1.8 13.1 %all_to_all.15.grads = bf16[4,2,32,1536]{3,2,1,0:T(8,128)(2,1)} all-to-all(bf16[4,2,32,1536]{3,2,1,0:T(8,128)(2,1)S(1)} %bitcast.7), channel_id=1, replica_groups=mesh['expert'=128,'dp'=4] {'dp'}, dimensions={0} | all-to-all | bytes 1572864 | tf_op jit(solution)/shard_map/all_to_all | solution.py:111
  14.9 2.2 %pack.1 = bf16[16,128,128]{2,1,0:T(8,128)(2,1)} custom-call(bf16[4,2,32,1536]{3,2,1,0:T(8,128)(2,1)} %all_to_all.15.grads, f32[1,32,1536]{2,1,0:T(8,128)} %master.3, f32[1,32,1536]{2,1,0:T(8,128)} %moment.3, f32[1,32,1536]{2,1,0:T(8,128)} %second.3), custom_call_target="tpu_custom_call" | custom-call | tf_op jit(solution)/shard_map/pack/pallas_call | solution.py:113
  17.2 1.4 %copy.13 = bf16[16,128,128]{2,0,1:T(8,128)(2,1)S(1)} copy(bf16[16,128,128]{2,1,0:T(8,128)(2,1)} %pack.1) | data formatting | bytes 1048576 | tf_op jit(solution)/shard_map/pack/pallas_call | solution.py:113
  18.5 42.2 %all_to_all.16 = bf16[16,128,128]{2,0,1:T(8,128)(2,1)S(1)} all-to-all(bf16[16,128,128]{2,0,1:T(8,128)(2,1)S(1)} %copy.13), channel_id=1, replica_groups=mesh['expert'=128,'dp'=4] {'expert'}, dimensions={1} | all-to-all | bytes 1048576 | tf_op jit(solution)/shard_map/all_to_all | solution.py:120
  60.7 0.9 %copy.14.pieces = bf16[16,128,128]{2,1,0:T(8,128)(2,1)} copy(bf16[16,128,128]{2,0,1:T(8,128)(2,1)S(1)} %all_to_all.16) | data formatting | bytes 1048576 | tf_op jit(solution)/shard_map/all_to_all | solution.py:120
  61.7 2.6 %update.1 = bf16[4,128,384]{2,1,0:T(8,128)(2,1)} custom-call(bf16[16,128,128]{2,1,0:T(8,128)(2,1)} %copy.14.pieces, s32[2,128]{1,0:T(2,128)} %bitcast.9, s32[2,128]{1,0:T(2,128)} %bitcast.10, s32[1,128]{1,0:T(1,128)} %bitcast.11), custom_call_target="tpu_custom_call" | custom-call | tf_op jit(solution)/shard_map/update/pallas_call | solution.py:121
  64.3 1.3 %copy.15 = bf16[4,128,384]{2,0,1:T(4,128)(2,1)S(1)} copy(bf16[4,128,384]{2,1,0:T(8,128)(2,1)} %update.1) | data formatting | bytes 786432 | tf_op jit(solution)/shard_map/update/pallas_call | solution.py:121
  65.6 23.1 %all_to_all.17 = bf16[4,128,384]{2,0,1:T(4,128)(2,1)S(1)} all-to-all(bf16[4,128,384]{2,0,1:T(4,128)(2,1)S(1)} %copy.15), channel_id=1, replica_groups=mesh['expert'=128,'dp'=4] {'expert'}, dimensions={1} | all-to-all | bytes 786432 | tf_op jit(solution)/shard_map/all_to_all | solution.py:128
  88.7 0.8 copy.16.pieces
  89.5 2.2 %finish.1 = (f32[1,32,1536]{2,1,0:T(8,128)}, f32[1,32,1536]{2,1,0:T(8,128)}, f32[1,32,1536]{2,1,0:T(8,128)}, bf16[2,32,1536]{2,1,0:T(8,128)(2,1)}) custom-call(bf16[4,128,384]{2,1,0:T(8,128)(2,1)} %copy.16.pieces, f32[1,32,1536]{2,1,0:T(8,128)} %master.3, f32[1,32,1536]{2,1,0:T(8,128)} %moment.3, f32[1,32,1536]{2,1,0:T(8,128)} %second.3), custom_call_target="tpu_custom_call" | custom-call | tf_op jit(solution)/shard_map/finish/pallas_call | solution.py:129

commit v2 on v1

v2 whole, which is shorter than its diff:
```python
import jax
import jax.numpy as jnp
from jax import lax
from jax.experimental import pallas as pl
from jax.experimental.pallas import tpu as pltpu
from jax.sharding import PartitionSpec as P

beta_first = 0.9
beta_second = 0.999
learn_rate = 0.02
weight_decay = 0.1
epsilon = 1e-08
scale_first = 1.0 - 0.9**40
scale_second = 1.0 - 0.999**40

LANES = 128


def adamw(master, moment, second, grad):
    new_moment = beta_first * moment + (1.0 - beta_first) * grad
    new_second = beta_second * second + (1.0 - beta_second) * grad * grad
    update = new_moment / scale_first / (jnp.sqrt(new_second / scale_second) + epsilon)
    new_master = master - learn_rate * (update + weight_decay * master)
    return new_master, new_moment, new_second


def pack_kernel(grads, master, moment, second, out):
    copies, slots, rows, cols = grads.shape
    devices, lines, _ = out.shape
    quarters = devices // rows
    tall = cols // quarters // LANES
    for q in range(quarters):
        blocks = []
        spans = [pl.ds((q * tall + i) * LANES, LANES) for i in range(tall)]
        for slot in range(slots):
            for span in spans:
                total = grads[0, slot, :, span].astype(jnp.float32)
                for copy in range(1, copies):
                    total = total + grads[copy, slot, :, span].astype(jnp.float32)
                blocks.append(total)
        for state in (master, moment, second):
            blocks += [state[0, :, span] for span in spans]
        blocks += [jnp.zeros((rows, LANES), jnp.float32)] * (lines - len(blocks))
        stacked = jnp.transpose(jnp.stack(blocks, 0), (1, 0, 2))
        out[q * rows : (q + 1) * rows] = stacked.astype(out.dtype)


def hot(rows, values):
    at = lax.broadcasted_iota(jnp.int32, (rows, values.shape[1]), 0)
    return (at == values).astype(jnp.bfloat16)


def dot(a, b, dims):
    return lax.dot_general(a, b, (dims, ((), ())), preferred_element_type=jnp.float32)


def update_kernel(pieces, old_place, new_place, owner_slot, out, arrived, leaving):
    slots, devices = old_place.shape
    lines = pieces.shape[1]
    lines_out = leaving.shape[0] // devices
    tall = lines_out // (slots + 1)
    experts = owner_slot.shape[1]
    arrived[...] = pieces[...].reshape(arrived.shape).astype(jnp.float32)

    def line(at):
        return arrived[pl.ds(at, devices, stride=lines), :]

    def leave(at, value):
        leaving[pl.ds(at, devices, stride=lines_out), :] = value

    owners = hot(devices, owner_slot[...])
    grad = jnp.zeros((devices, tall * LANES), jnp.float32)
    for slot in range(slots):
        held = hot(experts, old_place[slot : slot + 1, :])
        route = dot(owners, held, ((1,), (0,))).astype(jnp.bfloat16)
        part = [line(slot * tall + i).astype(jnp.bfloat16) for i in range(tall)]
        grad = grad + dot(route, jnp.concatenate(part, 1), ((1,), (0,)))
    fresh = []
    for i in range(tall):
        mine = grad[:, i * LANES : (i + 1) * LANES]
        master, moment, second = (line((slots + a) * tall + i) for a in range(3))
        fresh.append(adamw(master, moment, second, mine)[0].astype(jnp.bfloat16))
        leave(slots * tall + i, mine)
    fresh = jnp.concatenate(fresh, 1)
    for slot in range(slots):
        held = hot(experts, new_place[slot : slot + 1, :])
        route = dot(owners, held, ((1,), (0,))).astype(jnp.bfloat16)
        chosen = dot(route, fresh, ((0,), (0,)))
        for i in range(tall):
            leave(slot * tall + i, chosen[:, i * LANES : (i + 1) * LANES])
    for at in range((slots + 1) * tall, lines_out):
        leave(at, jnp.zeros((devices, LANES), jnp.float32))
    out[...] = leaving[...].astype(out.dtype).reshape(out.shape)


def finish_kernel(pieces, master, moment, second, new_master, new_moment, new_second, replicas, arrived):
    slots, rows, cols = replicas.shape
    devices = pieces.shape[0]
    lines = arrived.shape[0] // devices
    quarters = devices // rows
    tall = cols // quarters // LANES
    arrived[...] = pieces[...].reshape(arrived.shape).astype(jnp.float32)
    for q in range(quarters):
        for i in range(tall):
            there = pl.ds((q * tall + i) * LANES, LANES)

            def line(array, q=q, i=i):
                return arrived[pl.ds(q * rows * lines + array * tall + i, rows, stride=lines), :]

            for slot in range(slots):
                replicas[slot, :, there] = line(slot).astype(replicas.dtype)
            new_master[0, :, there], new_moment[0, :, there], new_second[0, :, there] = adamw(
                master[0, :, there], moment[0, :, there], second[0, :, there], line(slots)
            )


def call(kernel, name, outs, args, scratch=()):
    in_vmem = pl.BlockSpec(memory_space=pltpu.VMEM)
    args = [pltpu.with_memory_space_constraint(arg, pltpu.VMEM) for arg in args]
    return pl.pallas_call(
        kernel,
        out_shape=outs,
        in_specs=[in_vmem] * len(args),
        out_specs=[in_vmem] * len(outs) if isinstance(outs, list) else in_vmem,
        scratch_shapes=scratch,
        name=name,
    )(*args)


def on_device(grads, master, moment, second, old_place, new_place, owner_slot):
    devices = lax.axis_size("expert")
    copies = lax.axis_size("dp")
    _, slots, full_rows, cols = grads.shape
    rows = full_rows // copies
    tall = rows * cols // devices // LANES
    lines = -(-(slots + 3) * tall // 16) * 16
    pairs = -(-(slots + 1) * tall // 2)
    state = (master, moment, second)

    by_rows = grads.reshape(slots, copies, rows, cols).transpose(1, 0, 2, 3)
    mine = lax.all_to_all(by_rows, "dp", split_axis=0, concat_axis=0, tiled=True)
    packed = call(
        pack_kernel, "pack", pltpu.VMEM((devices, lines, LANES), jnp.bfloat16), (mine, *state)
    )
    pieces = lax.all_to_all(packed, "expert", split_axis=0, concat_axis=0, tiled=True)
    outbound = call(
        update_kernel,
        "update",
        pltpu.VMEM((devices, pairs, 2, LANES), jnp.bfloat16),
        (pieces, old_place.T, new_place.T, owner_slot[None, :]),
        [
            pltpu.VMEM((devices * lines, LANES), jnp.float32),
            pltpu.VMEM((devices * pairs * 2, LANES), jnp.float32),
        ],
    )
    received = lax.all_to_all(outbound, "expert", split_axis=0, concat_axis=0, tiled=True)
    return call(
        finish_kernel,
        "finish",
        [jax.ShapeDtypeStruct(master.shape, jnp.float32)] * 3
        + [jax.ShapeDtypeStruct((slots, rows, cols), jnp.bfloat16)],
        (received, *state),
        [pltpu.VMEM((devices * pairs * 2, LANES), jnp.float32)],
    )


def solution(mesh):
    placed = (
        P("dp", "expert", None, None),
        P("expert", "dp", None),
        P("expert", "dp", None),
        P("expert", "dp", None),
        P(),
        P(),
        P(),
    )
    return jax.shard_map(
        on_device,
        mesh=mesh,
        in_specs=placed,
        out_specs=(
            P("expert", "dp", None),
            P("expert", "dp", None),
            P("expert", "dp", None),
            P("expert", "dp", None),
        ),
        check_vma=False,
    )
```

time: 92.1 us -> 82.6 us (0.90)
  Pallas kernels: 7.09 us -> 2.63 us
  local copies, waits for them, and re-layouts: 5.58 us -> 1.9 us
  blocking collectives: 78.4 us -> 77.1 us
    pallas_call x3, Pallas kernels: 7.09 us -> 2.63 us  [call(): pl.pallas_call(kernel, out_shape=outs, in_specs=[in_vmem] * len(args), ou...]
    pallas_call x2 -> x0, local copies, waits for them, and re-layouts: 2.68 us -> none  [the longest x1 1.38 us: on_device(): pl.pallas_call(pack_kernel, out_shape=jax.ShapeDtypeStruct((lines, device...]
    all_to_all x2 -> x0, local copies, waits for them, and re-layouts: 1.71 us -> none  [the longest x1 0.93 us: on_device(): lax.all_to_all(packed, 'expert', split_axis=1, concat_axis=1, tiled=True)]
    all_to_all x2, blocking collectives: 65.3 us -> 64 us  [the longest x1 42.2 us: on_device(): lax.all_to_all(packed, 'expert', split_axis=0, concat_axis=0, tiled=True)]
where the time goes in v2:
time: 82.6 us; the launch traced here: 82.3 us
  blocking collectives  77.1 us (93%)
  Pallas kernels  2.63 us (3%)
  local copies, waits for them, and re-layouts  1.9 us (2%)
    all_to_all x1, blocking collectives, on_device(): lax.all_to_all(packed, 'expert', split_axis=0, concat_axis=0, tiled=True)  42.2 us
    all_to_all x1, blocking collectives, on_device(): lax.all_to_all(outbound, 'expert', split_axis=0, concat_axis=0, tiled=True)  21.8 us
    all_to_all x1, blocking collectives, on_device(): lax.all_to_all(by_rows, 'dp', split_axis=0, concat_axis=0, tiled=True)  13.1 us
    pallas_call x3, Pallas kernels, call(): pl.pallas_call(kernel, out_shape=outs, in_specs=[in_vmem] * len(args), ou...  2.63 us

profile of v2, /device:TPU:1, one launch (start us, length us, event | category | flops | bytes accessed | tf_op | source)
XLA Modules:
  0.0 82.3 jit_solution(17207867970021315622)
XLA Ops:
  0.6 1.2 %copy.13 = bf16[2,4,32,1536]{3,2,0,1:T(8,128)(2,1)S(1)} copy(bf16[2,4,32,1536]{3,2,1,0:T(8,128)(2,1)} %bitcast.11) | data formatting | bytes 1572864 | tf_op jit(solution)/shard_map/reshape | solution.py:140
  1.8 0.0 copy-start
  1.8 0.0 copy-start.1
  1.9 0.0 copy-start.2
  1.9 13.1 %all_to_all.15.grads = bf16[4,2,32,1536]{3,2,1,0:T(8,128)(2,1)S(1)} all-to-all(bf16[4,2,32,1536]{3,2,1,0:T(8,128)(2,1)S(1)} %bitcast.10), channel_id=1, replica_groups=mesh['expert'=128,'dp'=4] {'dp'}, dimensions={0} | all-to-all | bytes 1572864 | tf_op jit(solution)/shard_map/all_to_all | solution.py:141
  15.0 0.0 copy-done
  15.0 0.0 copy-done.1
  15.0 0.0 copy-done.2
  15.0 0.3 pack.1
  15.3 0.0 copy-start.4
  15.3 42.2 %all_to_all.16.pieces = bf16[128,16,128]{2,1,0:T(8,128)(2,1)S(1)} all-to-all(bf16[128,16,128]{2,1,0:T(8,128)(2,1)S(1)} %pack.1), channel_id=1, replica_groups=mesh['expert'=128,'dp'=4] {'expert'}, dimensions={0} | all-to-all | bytes 1048576 | tf_op jit(solution)/shard_map/all_to_all | solution.py:145
  57.5 0.0 copy-start.3
  57.5 0.0 copy-start.5
  57.5 0.0 copy-done.4
  57.5 0.7 copy-done.3
  58.2 0.0 copy-done.5
  58.2 1.0 %update.1 = bf16[128,5,2,128]{3,2,1,0:T(2,128)(2,1)S(1)} custom-call(bf16[128,16,128]{2,1,0:T(8,128)(2,1)S(1)} %all_to_all.16.pieces, s32[2,128]{1,0:T(2,128)S(1)} %bitcast.7, s32[2,128]{1,0:T(2,128)S(1)} %bitcast.8, s32[1,128]{1,0:T(1,128)S(1)} %bitcast.9), custom_call_target="tpu_custom_call" | custom-call | tf_op jit(solution)/shard_map/update/pallas_call | solution.py:120
  59.2 21.8 %all_to_all.17.pieces = bf16[128,5,2,128]{3,2,1,0:T(2,128)(2,1)S(1)} all-to-all(bf16[128,5,2,128]{3,2,1,0:T(2,128)(2,1)S(1)} %update.1), channel_id=1, replica_groups=mesh['expert'=128,'dp'=4] {'expert'}, dimensions={0} | all-to-all | bytes 655360 | tf_op jit(solution)/shard_map/all_to_all | solution.py:156
  81.0 1.3 %finish.1 = (f32[1,32,1536]{2,1,0:T(8,128)}, f32[1,32,1536]{2,1,0:T(8,128)}, f32[1,32,1536]{2,1,0:T(8,128)}, bf16[2,32,1536]{2,1,0:T(8,128)(2,1)}) custom-call(bf16[128,5,2,128]{3,2,1,0:T(2,128)(2,1)S(1)} %all_to_all.17.pieces, f32[1,32,1536]{2,1,0:T(8,128)S(1)} %copy-done, f32[1,32,1536]{2,1,0:T(8,128)S(1)} %copy-done.1, f32[1,32,1536]{2,1,0:T(8,128)S(1)} %copy-done.2), custom_call_target="tpu_custom_call" | custom-call | tf_op jit(solution)/shard_map/finish/pallas_call | solution.py:120
Async XLA Ops:
  1.8 13.2 %copy-start = (f32[1,32,1536]{2,1,0:T(8,128)S(1)}, f32[1,32,1536]{2,1,0:T(8,128)}, u32[]{:S(2)}) copy-start(f32[1,32,1536]{2,1,0:T(8,128)} %master.3) | copy-start | bytes 589828
  1.8 13.1 %copy-start.1 = (f32[1,32,1536]{2,1,0:T(8,128)S(1)}, f32[1,32,1536]{2,1,0:T(8,128)}, u32[]{:S(2)}) copy-start(f32[1,32,1536]{2,1,0:T(8,128)} %moment.3) | copy-start | bytes 589828
  1.9 13.1 %copy-start.2 = (f32[1,32,1536]{2,1,0:T(8,128)S(1)}, f32[1,32,1536]{2,1,0:T(8,128)}, u32[]{:S(2)}) copy-start(f32[1,32,1536]{2,1,0:T(8,128)} %second.3) | copy-start | bytes 589828
  15.3 42.2 %copy-start.4 = (s32[128,2]{0,1:T(2,128)S(1)}, s32[128,2]{0,1:T(2,128)}, u32[]{:S(2)}) copy-start(s32[128,2]{0,1:T(2,128)} %param.12) | copy-start | bytes 3076
  57.5 0.7 copy-start.3
  57.5 0.7 copy-start.5

commit v3 on v2

--- a/solution.py
+++ b/solution.py
@@ -22,6 +22,43 @@
     update = new_moment / scale_first / (jnp.sqrt(new_second / scale_second) + epsilon)
     new_master = master - learn_rate * (update + weight_decay * master)
     return new_master, new_moment, new_second
+
+
+def hot(rows, values):
+    at = lax.broadcasted_iota(jnp.int32, (rows, values.shape[1]), 0)
+    return (at == values).astype(jnp.bfloat16)
+
+
+def dot(a, b, dims):
+    return lax.dot_general(a, b, (dims, ((), ())), preferred_element_type=jnp.float32)
+
+
+def load_kernel(grads, places, by_rows, routes, held_places, sems):
+    slots, copies = grads.shape[:2]
+    index_copies = [
+        pltpu.make_async_copy(place, held, sems.at[slots * copies + at])
+        for at, (place, held) in enumerate(zip(places, held_places))
+    ]
+    grad_copies = [
+        pltpu.make_async_copy(
+            grads.at[slot, copy], by_rows.at[copy, slot], sems.at[slot * copies + copy]
+        )
+        for slot in range(slots)
+        for copy in range(copies)
+    ]
+    for each in index_copies + grad_copies:
+        each.start()
+    for each in index_copies:
+        each.wait()
+    old_place, new_place, owner_slot = held_places
+    _, owner_count, _ = routes.shape
+    owners = hot(owner_count, owner_slot[...])
+    for at, place in enumerate((old_place, new_place)):
+        for slot in range(slots):
+            held = hot(owner_slot.shape[1], place[slot : slot + 1, :])
+            routes[at * slots + slot] = dot(owners, held, ((1,), (0,))).astype(routes.dtype)
+    for each in grad_copies:
+        each.wait()
 
 
 def pack_kernel(grads, master, moment, second, out):
@@ -45,47 +82,30 @@
         out[q * rows : (q + 1) * rows] = stacked.astype(out.dtype)
 
 
-def hot(rows, values):
-    at = lax.broadcasted_iota(jnp.int32, (rows, values.shape[1]), 0)
-    return (at == values).astype(jnp.bfloat16)
-
-
-def dot(a, b, dims):
-    return lax.dot_general(a, b, (dims, ((), ())), preferred_element_type=jnp.float32)
-
-
-def update_kernel(pieces, old_place, new_place, owner_slot, out, arrived, leaving):
-    slots, devices = old_place.shape
-    lines = pieces.shape[1]
+def update_kernel(pieces, routes, out, leaving):
+    slots, devices = routes.shape[0] // 2, routes.shape[2]
     lines_out = leaving.shape[0] // devices
     tall = lines_out // (slots + 1)
-    experts = owner_slot.shape[1]
-    arrived[...] = pieces[...].reshape(arrived.shape).astype(jnp.float32)
-
-    def line(at):
-        return arrived[pl.ds(at, devices, stride=lines), :]
+    arrived = jnp.transpose(pieces[...], (1, 0, 2))
 
     def leave(at, value):
         leaving[pl.ds(at, devices, stride=lines_out), :] = value
 
-    owners = hot(devices, owner_slot[...])
     grad = jnp.zeros((devices, tall * LANES), jnp.float32)
     for slot in range(slots):
-        held = hot(experts, old_place[slot : slot + 1, :])
-        route = dot(owners, held, ((1,), (0,))).astype(jnp.bfloat16)
-        part = [line(slot * tall + i).astype(jnp.bfloat16) for i in range(tall)]
-        grad = grad + dot(route, jnp.concatenate(part, 1), ((1,), (0,)))
+        part = [arrived[slot * tall + i] for i in range(tall)]
+        grad = grad + dot(routes[slot], jnp.concatenate(part, 1), ((1,), (0,)))
     fresh = []
     for i in range(tall):
         mine = grad[:, i * LANES : (i + 1) * LANES]
-        master, moment, second = (line((slots + a) * tall + i) for a in range(3))
+        master, moment, second = (
+            arrived[(slots + a) * tall + i].astype(jnp.float32) for a in range(3)
+        )
         fresh.append(adamw(master, moment, second, mine)[0].astype(jnp.bfloat16))
         leave(slots * tall + i, mine)
     fresh = jnp.concatenate(fresh, 1)
     for slot in range(slots):
-        held = hot(experts, new_place[slot : slot + 1, :])
-        route = dot(owners, held, ((1,), (0,))).astype(jnp.bfloat16)
-        chosen = dot(route, fresh, ((0,), (0,)))
+        chosen = dot(routes[slots + slot], fresh, ((0,), (0,)))
         for i in range(tall):
             leave(slot * tall + i, chosen[:, i * LANES : (i + 1) * LANES])
     for at in range((slots + 1) * tall, lines_out):
@@ -127,6 +147,30 @@
     )(*args)
 
 
+def load(grads, old_place, new_place, owner_slot):
+    slots, copies, rows, cols = grads.shape
+    devices = old_place.shape[0]
+    places = (old_place.T, new_place.T, owner_slot[None, :])
+    in_vmem = pl.BlockSpec(memory_space=pltpu.VMEM)
+    anywhere = pl.BlockSpec(memory_space=pl.ANY)
+
+    def kernel(grads, *refs):
+        load_kernel(grads, refs[:3], refs[3], refs[4], refs[5:8], refs[8])
+
+    return pl.pallas_call(
+        kernel,
+        out_shape=[
+            pltpu.VMEM((copies, slots, rows, cols), grads.dtype),
+            pltpu.VMEM((2 * slots, devices, devices), jnp.bfloat16),
+        ],
+        in_specs=[anywhere] * 4,
+        out_specs=[in_vmem] * 2,
+        scratch_shapes=[pltpu.VMEM(place.shape, place.dtype) for place in places]
+        + [pltpu.SemaphoreType.DMA((slots * copies + 3,))],
+        name="load",
+    )(grads, *places)
+
+
 def on_device(grads, master, moment, second, old_place, new_place, owner_slot):
     devices = lax.axis_size("expert")
     copies = lax.axis_size("dp")
@@ -137,7 +181,7 @@
     pairs = -(-(slots + 1) * tall // 2)
     state = (master, moment, second)
 
-    by_rows = grads.reshape(slots, copies, rows, cols).transpose(1, 0, 2, 3)
+    by_rows, routes = load(grads.reshape(slots, copies, rows, cols), old_place, new_place, owner_slot)
     mine = lax.all_to_all(by_rows, "dp", split_axis=0, concat_axis=0, tiled=True)
     packed = call(
         pack_kernel, "pack", pltpu.VMEM((devices, lines, LANES), jnp.bfloat16), (mine, *state)
@@ -147,11 +191,8 @@
         update_kernel,
         "update",
         pltpu.VMEM((devices, pairs, 2, LANES), jnp.bfloat16),
-        (pieces, old_place.T, new_place.T, owner_slot[None, :]),
-        [
-            pltpu.VMEM((devices * lines, LANES), jnp.float32),
-            pltpu.VMEM((devices * pairs * 2, LANES), jnp.float32),
-        ],
+        (pieces, routes),
+        [pltpu.VMEM((devices * pairs * 2, LANES), jnp.float32)],
     )
     received = lax.all_to_all(outbound, "expert", split_axis=0, concat_axis=0, tiled=True)
     return call(

time: 82.6 us -> 81.7 us (0.989)
  local copies, waits for them, and re-layouts: 1.9 us -> 0.02 us
  Pallas kernels: 2.63 us -> 3.66 us
    pallas_call x0 -> x1, Pallas kernels: none -> 1.35 us  [load(): pl.pallas_call(kernel, out_shape=[pltpu.VMEM((copies, slots, rows, cols),...]
    reshape x1 -> x0, local copies, waits for them, and re-layouts: 1.2 us -> none  [on_device(): by_rows = grads.reshape(slots, copies, rows, cols).transpose(1, 0, 2, 3)]
where the time goes in v3:
time: 81.7 us; the launch traced here: 81.5 us
  blocking collectives  77.1 us (94%)
  Pallas kernels  3.66 us (4%)
    all_to_all x1, blocking collectives, on_device(): lax.all_to_all(packed, 'expert', split_axis=0, concat_axis=0, tiled=True)  42.2 us
    all_to_all x1, blocking collectives, on_device(): lax.all_to_all(outbound, 'expert', split_axis=0, concat_axis=0, tiled=True)  21.8 us
    all_to_all x1, blocking collectives, on_device(): lax.all_to_all(by_rows, 'dp', split_axis=0, concat_axis=0, tiled=True)  13.1 us
    pallas_call x3, Pallas kernels, call(): pl.pallas_call(kernel, out_shape=outs, in_specs=[in_vmem] * len(args), ou...  2.31 us

profile of v3, /device:TPU:1, one launch (start us, length us, event | category | flops | bytes accessed | tf_op | source)
XLA Modules:
  0.0 81.5 jit_solution(16437258497495304915)
XLA Ops:
  0.6 1.3 %load.1 = (bf16[4,2,32,1536]{3,2,1,0:T(8,128)(2,1)S(1)}, bf16[4,128,128]{2,1,0:T(8,128)(2,1)S(1)}) custom-call(bf16[2,4,32,1536]{3,2,1,0:T(8,128)(2,1)} %bitcast.4, s32[2,128]{1,0:T(2,128)} %bitcast.5, s32[2,128]{1,0:T(2,128)} %bitcast.6, s32[1,128]{1,0:T(1,128)} %bitcast.7), custom_call_target="tpu_custom_call" | custom-call | tf_op jit(solution)/shard_map/load/pallas_call | solution.py:160
  2.0 0.0 copy-start
  2.0 0.0 copy-start.1
  2.0 0.0 copy-start.2
  2.0 13.1 %all_to_all.15.grads = bf16[4,2,32,1536]{3,2,1,0:T(8,128)(2,1)S(1)} all-to-all(bf16[4,2,32,1536]{3,2,1,0:T(8,128)(2,1)S(1)} %get-tuple-element.6), channel_id=1, replica_groups=mesh['expert'=128,'dp'=4] {'dp'}, dimensions={0} | all-to-all | bytes 1572864 | tf_op jit(solution)/shard_map/all_to_all | solution.py:185
  15.1 0.0 copy-done
  15.1 0.0 copy-done.1
  15.1 0.0 copy-done.2
  15.1 0.3 pack.1
  15.4 42.2 %all_to_all.16.pieces = bf16[128,16,128]{2,1,0:T(8,128)(2,1)S(1)} all-to-all(bf16[128,16,128]{2,1,0:T(8,128)(2,1)S(1)} %pack.1), channel_id=1, replica_groups=mesh['expert'=128,'dp'=4] {'expert'}, dimensions={0} | all-to-all | bytes 1048576 | tf_op jit(solution)/shard_map/all_to_all | solution.py:189
  57.6 0.7 update.1
  58.3 21.8 %all_to_all.17.pieces = bf16[128,5,2,128]{3,2,1,0:T(2,128)(2,1)S(1)} all-to-all(bf16[128,5,2,128]{3,2,1,0:T(2,128)(2,1)S(1)} %update.1), channel_id=1, replica_groups=mesh['expert'=128,'dp'=4] {'expert'}, dimensions={0} | all-to-all | bytes 655360 | tf_op jit(solution)/shard_map/all_to_all | solution.py:197
  80.1 1.3 %finish.1 = (f32[1,32,1536]{2,1,0:T(8,128)}, f32[1,32,1536]{2,1,0:T(8,128)}, f32[1,32,1536]{2,1,0:T(8,128)}, bf16[2,32,1536]{2,1,0:T(8,128)(2,1)}) custom-call(bf16[128,5,2,128]{3,2,1,0:T(2,128)(2,1)S(1)} %all_to_all.17.pieces, f32[1,32,1536]{2,1,0:T(8,128)S(1)} %copy-done, f32[1,32,1536]{2,1,0:T(8,128)S(1)} %copy-done.1, f32[1,32,1536]{2,1,0:T(8,128)S(1)} %copy-done.2), custom_call_target="tpu_custom_call" | custom-call | tf_op jit(solution)/shard_map/finish/pallas_call | solution.py:140
Async XLA Ops:
  2.0 13.2 %copy-start = (f32[1,32,1536]{2,1,0:T(8,128)S(1)}, f32[1,32,1536]{2,1,0:T(8,128)}, u32[]{:S(2)}) copy-start(f32[1,32,1536]{2,1,0:T(8,128)} %master.3) | copy-start | bytes 589828
  2.0 13.1 %copy-start.1 = (f32[1,32,1536]{2,1,0:T(8,128)S(1)}, f32[1,32,1536]{2,1,0:T(8,128)}, u32[]{:S(2)}) copy-start(f32[1,32,1536]{2,1,0:T(8,128)} %moment.3) | copy-start | bytes 589828
  2.0 13.1 %copy-start.2 = (f32[1,32,1536]{2,1,0:T(8,128)S(1)}, f32[1,32,1536]{2,1,0:T(8,128)}, u32[]{:S(2)}) copy-start(f32[1,32,1536]{2,1,0:T(8,128)} %second.3) | copy-start | bytes 589828

commit v4 on v3

--- a/solution.py
+++ b/solution.py
@@ -33,7 +33,7 @@
     return lax.dot_general(a, b, (dims, ((), ())), preferred_element_type=jnp.float32)
 
 
-def load_kernel(grads, places, by_rows, routes, held_places, sems):
+def load_kernel(me, grads, places, by_rows, routes, held_places, sems):
     slots, copies = grads.shape[:2]
     index_copies = [
         pltpu.make_async_copy(place, held, sems.at[slots * copies + at])
@@ -41,10 +41,12 @@
     ]
     grad_copies = [
         pltpu.make_async_copy(
-            grads.at[slot, copy], by_rows.at[copy, slot], sems.at[slot * copies + copy]
+            grads.at[slot, lax.rem(me + turn, copies)],
+            by_rows[turn].at[slot],
+            sems.at[slot * copies + turn],
         )
         for slot in range(slots)
-        for copy in range(copies)
+        for turn in range(copies)
     ]
     for each in index_copies + grad_copies:
         each.start()
@@ -61,8 +63,10 @@
         each.wait()
 
 
-def pack_kernel(grads, master, moment, second, out):
-    copies, slots, rows, cols = grads.shape
+def pack_kernel(*refs):
+    *grads, master, moment, second, out = refs
+    copies = len(grads)
+    slots, rows, cols = grads[0].shape
     devices, lines, _ = out.shape
     quarters = devices // rows
     tall = cols // quarters // LANES
@@ -71,9 +75,9 @@
         spans = [pl.ds((q * tall + i) * LANES, LANES) for i in range(tall)]
         for slot in range(slots):
             for span in spans:
-                total = grads[0, slot, :, span].astype(jnp.float32)
+                total = grads[0][slot, :, span].astype(jnp.float32)
                 for copy in range(1, copies):
-                    total = total + grads[copy, slot, :, span].astype(jnp.float32)
+                    total = total + grads[copy][slot, :, span].astype(jnp.float32)
                 blocks.append(total)
         for state in (master, moment, second):
             blocks += [state[0, :, span] for span in spans]
@@ -155,16 +159,17 @@
     anywhere = pl.BlockSpec(memory_space=pl.ANY)
 
     def kernel(grads, *refs):
-        load_kernel(grads, refs[:3], refs[3], refs[4], refs[5:8], refs[8])
+        me = lax.axis_index("dp")
+        load_kernel(me, grads, refs[:3], refs[3:7], refs[7], refs[8:11], refs[11])
 
     return pl.pallas_call(
         kernel,
         out_shape=[
-            pltpu.VMEM((copies, slots, rows, cols), grads.dtype),
+            *[pltpu.VMEM((slots, rows, cols), grads.dtype)] * copies,
             pltpu.VMEM((2 * slots, devices, devices), jnp.bfloat16),
         ],
         in_specs=[anywhere] * 4,
-        out_specs=[in_vmem] * 2,
+        out_specs=[in_vmem] * (copies + 1),
         scratch_shapes=[pltpu.VMEM(place.shape, place.dtype) for place in places]
         + [pltpu.SemaphoreType.DMA((slots * copies + 3,))],
         name="load",
@@ -181,10 +186,13 @@
     pairs = -(-(slots + 1) * tall // 2)
     state = (master, moment, second)
 
-    by_rows, routes = load(grads.reshape(slots, copies, rows, cols), old_place, new_place, owner_slot)
-    mine = lax.all_to_all(by_rows, "dp", split_axis=0, concat_axis=0, tiled=True)
+    *by_rows, routes = load(grads.reshape(slots, copies, rows, cols), old_place, new_place, owner_slot)
+    mine = [by_rows[0]]
+    for turn in sorted(range(1, copies), key=lambda d: abs(copies - 2 * d)):
+        moves = [(i, (i + turn) % copies) for i in range(copies)]
+        mine.append(lax.ppermute(by_rows[turn], "dp", moves))
     packed = call(
-        pack_kernel, "pack", pltpu.VMEM((devices, lines, LANES), jnp.bfloat16), (mine, *state)
+        pack_kernel, "pack", pltpu.VMEM((devices, lines, LANES), jnp.bfloat16), (*mine, *state)
     )
     pieces = lax.all_to_all(packed, "expert", split_axis=0, concat_axis=0, tiled=True)
     outbound = call(

time: 81.7 us -> 81 us (level)
  blocking collectives: 77.1 us -> 61.6 us
  starting transfers between devices: 0 us -> 12 us
  waiting for transfers between devices: 0 us -> 2.58 us
    all_to_all x1 -> x0, blocking collectives: 13.1 us -> none  [on_device(): lax.all_to_all(by_rows, 'dp', split_axis=0, concat_axis=0, tiled=True)]
    ppermute x0 -> x3, starting transfers between devices: none -> 12 us  [on_device(): mine.append(lax.ppermute(by_rows[turn], 'dp', moves))]
    ppermute x0 -> x3, waiting for transfers between devices: none -> 2.58 us  [on_device(): mine.append(lax.ppermute(by_rows[turn], 'dp', moves))]
    all_to_all x1, blocking collectives: 42.2 us -> 39.8 us  [on_device(): lax.all_to_all(packed, 'expert', split_axis=0, concat_axis=0, tiled=True)]
  transfers between devices with their start and end apart: 0 -> 3, of which waited for: 0 -> 2; matrix products, arithmetic and copies ran while one was open for 0% -> 0% of each run, Pallas kernels for 0% -> 0%
where the time goes in v4:
time: 81 us; the launch traced here: 80.6 us
  blocking collectives  61.6 us (76%)
  starting transfers between devices  12 us (15%)
  Pallas kernels  3.73 us (5%)
  waiting for transfers between devices  2.58 us (3%)
    all_to_all x1, blocking collectives, on_device(): lax.all_to_all(packed, 'expert', split_axis=0, concat_axis=0, tiled=True)  39.8 us
    all_to_all x1, blocking collectives, on_device(): lax.all_to_all(outbound, 'expert', split_axis=0, concat_axis=0, tiled=True)  21.8 us
    ppermute x3, starting transfers between devices, on_device(): mine.append(lax.ppermute(by_rows[turn], 'dp', moves))  12 us
    ppermute x3, waiting for transfers between devices, on_device(): mine.append(lax.ppermute(by_rows[turn], 'dp', moves))  2.58 us
    pallas_call x3, Pallas kernels, call(): pl.pallas_call(kernel, out_shape=outs, in_specs=[in_vmem] * len(args), ou...  2.31 us
  transfers between devices with their start and end apart: 3, of which 2 were waited for; matrix products, arithmetic and copies ran while one was open for 0% of the time, Pallas kernels for 0%

profile of v4, /device:TPU:1, one launch (start us, length us, event | category | flops | bytes accessed | tf_op | source)
XLA Modules:
  0.0 80.6 jit_solution(13307051296044912340)
XLA Ops:
  0.6 0.0 copy-start
  0.6 0.0 copy-start.1
  0.7 0.0 copy-start.2
  0.7 1.4 %load.1 = (bf16[2,32,1536]{2,1,0:T(8,128)(2,1)S(1)}, bf16[2,32,1536]{2,1,0:T(8,128)(2,1)S(1)}, bf16[2,32,1536]{2,1,0:T(8,128)(2,1)S(1)}, bf16[2,32,1536]{2,1,0:T(8,128)(2,1)S(1)}, bf16[4,128,128]{2,1,0:T(8,128)(2,1)S(1)}) custom-call(bf16[2,4,32,1536]{3,2,1,0:T(8,128)(2,1)} %bitcast.4, s32[2,128]{1,0:T(2,128)} %bitcast.5, s32[2,128]{1,0:T(2,128)} %bitcast.6, ...), custom_call_target="tpu_custom_call" | custom-call | tf_op jit(solution)/shard_map/load/pallas_call | solution.py:165
  2.1 5.5 %collective-permute-start = (bf16[2,32,1536]{2,1,0:T(8,128)(2,1)S(1)}, bf16[2,32,1536]{2,1,0:T(8,128)(2,1)S(1)}, u32[]{:S(2)}, u32[]{:S(2)}) collective-permute-start(bf16[2,32,1536]{2,1,0:T(8,128)(2,1)S(1)} %get-tuple-element.10), channel_id=1, source_target_pairs={{0,2},{1,3},{2,0},{3,1},{4,6},{5,7},{6,4},{7,5},{8,10},{9,11},{10,... | collective-permute-start | bytes 589832 | tf_op jit(solution)/shard_map/ppermute | solution.py:193
  7.6 2.2 %collective-permute-start.1 = (bf16[2,32,1536]{2,1,0:T(8,128)(2,1)S(1)}, bf16[2,32,1536]{2,1,0:T(8,128)(2,1)S(1)}, u32[]{:S(2)}, u32[]{:S(2)}) collective-permute-start(bf16[2,32,1536]{2,1,0:T(8,128)(2,1)S(1)} %get-tuple-element.11), channel_id=1, source_target_pairs={{0,1},{1,2},{2,3},{3,0},{4,5},{5,6},{6,7},{7,4},{8,9},{9,10},{10,1... | collective-permute-start | bytes 589832 | tf_op jit(solution)/shard_map/ppermute | solution.py:193
  9.8 4.3 %collective-permute-start.2 = (bf16[2,32,1536]{2,1,0:T(8,128)(2,1)S(1)}, bf16[2,32,1536]{2,1,0:T(8,128)(2,1)S(1)}, u32[]{:S(2)}, u32[]{:S(2)}) collective-permute-start(bf16[2,32,1536]{2,1,0:T(8,128)(2,1)S(1)} %get-tuple-element.12), channel_id=1, source_target_pairs={{0,3},{1,0},{2,1},{3,2},{4,7},{5,4},{6,5},{7,6},{8,11},{9,8},{10,9... | collective-permute-start | bytes 589832 | tf_op jit(solution)/shard_map/ppermute | solution.py:193
  14.1 0.0 collective-permute-done.refs_1_
  14.1 1.1 %collective-permute-done.1.refs_2_ = bf16[2,32,1536]{2,1,0:T(8,128)(2,1)S(1)} collective-permute-done((bf16[2,32,1536]{2,1,0:T(8,128)(2,1)S(1)}, bf16[2,32,1536]{2,1,0:T(8,128)(2,1)S(1)}, u32[]{:S(2)}, u32[]{:S(2)}) %collective-permute-start.1) | collective-permute-done | bytes 196640 | tf_op jit(solution)/shard_map/ppermute | solution.py:193
  15.2 1.5 %collective-permute-done.2.refs_3_ = bf16[2,32,1536]{2,1,0:T(8,128)(2,1)S(1)} collective-permute-done((bf16[2,32,1536]{2,1,0:T(8,128)(2,1)S(1)}, bf16[2,32,1536]{2,1,0:T(8,128)(2,1)S(1)}, u32[]{:S(2)}, u32[]{:S(2)}) %collective-permute-start.2) | collective-permute-done | bytes 196640 | tf_op jit(solution)/shard_map/ppermute | solution.py:193
  16.7 0.0 copy-done
  16.7 0.0 copy-done.1
  16.7 0.0 copy-done.2
  16.7 0.3 pack.1
  17.0 39.8 %all_to_all.10.pieces = bf16[128,16,128]{2,1,0:T(8,128)(2,1)S(1)} all-to-all(bf16[128,16,128]{2,1,0:T(8,128)(2,1)S(1)} %pack.1), channel_id=1, replica_groups=mesh['expert'=128,'dp'=4] {'expert'}, dimensions={0} | all-to-all | bytes 1048576 | tf_op jit(solution)/shard_map/all_to_all | solution.py:197
  56.8 0.7 update.1
  57.5 21.8 %all_to_all.11.pieces = bf16[128,5,2,128]{3,2,1,0:T(2,128)(2,1)S(1)} all-to-all(bf16[128,5,2,128]{3,2,1,0:T(2,128)(2,1)S(1)} %update.1), channel_id=1, replica_groups=mesh['expert'=128,'dp'=4] {'expert'}, dimensions={0} | all-to-all | bytes 655360 | tf_op jit(solution)/shard_map/all_to_all | solution.py:205
  79.3 1.3 %finish.1 = (f32[1,32,1536]{2,1,0:T(8,128)}, f32[1,32,1536]{2,1,0:T(8,128)}, f32[1,32,1536]{2,1,0:T(8,128)}, bf16[2,32,1536]{2,1,0:T(8,128)(2,1)}) custom-call(bf16[128,5,2,128]{3,2,1,0:T(2,128)(2,1)S(1)} %all_to_all.11.pieces, f32[1,32,1536]{2,1,0:T(8,128)S(1)} %copy-done, f32[1,32,1536]{2,1,0:T(8,128)S(1)} %copy-done.1, f32[1,32,1536]{2,1,0:T(8,128)S(1)} %copy-done.2), custom_call_target="tpu_custom_call" | custom-call | tf_op jit(solution)/shard_map/finish/pallas_call | solution.py:144
Async XLA Ops:
  0.6 16.1 %copy-start = (f32[1,32,1536]{2,1,0:T(8,128)S(1)}, f32[1,32,1536]{2,1,0:T(8,128)}, u32[]{:S(2)}) copy-start(f32[1,32,1536]{2,1,0:T(8,128)} %master.1) | copy-start | bytes 589828
  0.6 16.0 %copy-start.1 = (f32[1,32,1536]{2,1,0:T(8,128)S(1)}, f32[1,32,1536]{2,1,0:T(8,128)}, u32[]{:S(2)}) copy-start(f32[1,32,1536]{2,1,0:T(8,128)} %moment.1) | copy-start | bytes 589828
  0.7 16.0 %copy-start.2 = (f32[1,32,1536]{2,1,0:T(8,128)S(1)}, f32[1,32,1536]{2,1,0:T(8,128)}, u32[]{:S(2)}) copy-start(f32[1,32,1536]{2,1,0:T(8,128)} %second.1) | copy-start | bytes 589828
  2.1 12.0 %collective-permute-start = (bf16[2,32,1536]{2,1,0:T(8,128)(2,1)S(1)}, bf16[2,32,1536]{2,1,0:T(8,128)(2,1)S(1)}, u32[]{:S(2)}, u32[]{:S(2)}) collective-permute-start(bf16[2,32,1536]{2,1,0:T(8,128)(2,1)S(1)} %get-tuple-element.10), channel_id=1, source_target_pairs={{0,2},{1,3},{2,0},{3,1},{4,6},{5,7},{6,4},{7,5},{8,10},{9,11},{10,... | collective-permute-start | bytes 589832 | tf_op jit(solution)/shard_map/ppermute | solution.py:193
  7.6 7.6 %collective-permute-start.1 = (bf16[2,32,1536]{2,1,0:T(8,128)(2,1)S(1)}, bf16[2,32,1536]{2,1,0:T(8,128)(2,1)S(1)}, u32[]{:S(2)}, u32[]{:S(2)}) collective-permute-start(bf16[2,32,1536]{2,1,0:T(8,128)(2,1)S(1)} %get-tuple-element.11), channel_id=1, source_target_pairs={{0,1},{1,2},{2,3},{3,0},{4,5},{5,6},{6,7},{7,4},{8,9},{9,10},{10,1... | collective-permute-start | bytes 589832 | tf_op jit(solution)/shard_map/ppermute | solution.py:193
  9.8 6.9 %collective-permute-start.2 = (bf16[2,32,1536]{2,1,0:T(8,128)(2,1)S(1)}, bf16[2,32,1536]{2,1,0:T(8,128)(2,1)S(1)}, u32[]{:S(2)}, u32[]{:S(2)}) collective-permute-start(bf16[2,32,1536]{2,1,0:T(8,128)(2,1)S(1)} %get-tuple-element.12), channel_id=1, source_target_pairs={{0,3},{1,0},{2,1},{3,2},{4,7},{5,4},{6,5},{7,6},{8,11},{9,8},{10,9... | collective-permute-start | bytes 589832 | tf_op jit(solution)/shard_map/ppermute | solution.py:193

commit v5 on v4

--- a/solution.py
+++ b/solution.py
@@ -33,7 +33,14 @@
     return lax.dot_general(a, b, (dims, ((), ())), preferred_element_type=jnp.float32)
 
 
-def load_kernel(me, grads, places, by_rows, routes, held_places, sems):
+def turns(copies, odd):
+    return sorted(
+        range(copies),
+        key=lambda d: (d > 0, -min(d, copies - d), d if not odd else -d),
+    )
+
+
+def load_kernel(me, turned, grads, places, by_rows, routes, held_places, sems):
     slots, copies = grads.shape[:2]
     index_copies = [
         pltpu.make_async_copy(place, held, sems.at[slots * copies + at])
@@ -42,11 +49,11 @@
     grad_copies = [
         pltpu.make_async_copy(
             grads.at[slot, lax.rem(me + turn, copies)],
-            by_rows[turn].at[slot],
-            sems.at[slot * copies + turn],
+            by_rows[n].at[slot],
+            sems.at[slot * copies + n],
         )
         for slot in range(slots)
-        for turn in range(copies)
+        for n, turn in enumerate(turned)
     ]
     for each in index_copies + grad_copies:
         each.start()
@@ -160,7 +167,9 @@
 
     def kernel(grads, *refs):
         me = lax.axis_index("dp")
-        load_kernel(me, grads, refs[:3], refs[3:7], refs[7], refs[8:11], refs[11])
+        odd = lax.rem(lax.axis_index("expert"), 2)
+        turned = [a + odd * (b - a) for a, b in zip(turns(copies, 0), turns(copies, 1))]
+        load_kernel(me, turned, grads, refs[:3], refs[3:7], refs[7], refs[8:11], refs[11])
 
     return pl.pallas_call(
         kernel,
@@ -188,9 +197,13 @@
 
     *by_rows, routes = load(grads.reshape(slots, copies, rows, cols), old_place, new_place, owner_slot)
     mine = [by_rows[0]]
-    for turn in sorted(range(1, copies), key=lambda d: abs(copies - 2 * d)):
-        moves = [(i, (i + turn) % copies) for i in range(copies)]
-        mine.append(lax.ppermute(by_rows[turn], "dp", moves))
+    for n in range(1, copies):
+        moves = [
+            (k * copies + i, k * copies + (i + turns(copies, k % 2)[n]) % copies)
+            for k in range(devices)
+            for i in range(copies)
+        ]
+        mine.append(lax.ppermute(by_rows[n], ("expert", "dp"), moves))
     packed = call(
         pack_kernel, "pack", pltpu.VMEM((devices, lines, LANES), jnp.bfloat16), (*mine, *state)
     )

time: 81 us -> 80.6 us (level)
  waiting for transfers between devices: 2.58 us -> 8.76 us
  blocking collectives: 61.6 us -> 56.3 us
  starting transfers between devices: 12 us -> 10.8 us
    ppermute x3, waiting for transfers between devices: 2.58 us -> 8.76 us  [on_device(): mine.append(lax.ppermute(by_rows[n], ('expert', 'dp'), moves))]
    all_to_all x1, blocking collectives: 39.8 us -> 34.5 us  [on_device(): lax.all_to_all(packed, 'expert', split_axis=0, concat_axis=0, tiled=True)]
    ppermute x3, starting transfers between devices: 12 us -> 10.8 us  [on_device(): mine.append(lax.ppermute(by_rows[n], ('expert', 'dp'), moves))]
where the time goes in v5:
time: 80.6 us; the launch traced here: 80.3 us
  blocking collectives  56.3 us (70%)
  starting transfers between devices  10.8 us (13%)
  waiting for transfers between devices  8.76 us (11%)
  Pallas kernels  3.73 us (5%)
    all_to_all x1, blocking collectives, on_device(): lax.all_to_all(packed, 'expert', split_axis=0, concat_axis=0, tiled=True)  34.5 us
    all_to_all x1, blocking collectives, on_device(): lax.all_to_all(outbound, 'expert', split_axis=0, concat_axis=0, tiled=True)  21.8 us
    ppermute x3, starting transfers between devices, on_device(): mine.append(lax.ppermute(by_rows[n], ('expert', 'dp'), moves))  10.8 us
    ppermute x3, waiting for transfers between devices, on_device(): mine.append(lax.ppermute(by_rows[n], ('expert', 'dp'), moves))  8.76 us
    pallas_call x3, Pallas kernels, call(): pl.pallas_call(kernel, out_shape=outs, in_specs=[in_vmem] * len(args), ou...  2.31 us
  transfers between devices with their start and end apart: 3, of which 2 were waited for; matrix products, arithmetic and copies ran while one was open for 0% of the time, Pallas kernels for 0%

profile of v5, /device:TPU:1, one launch (start us, length us, event | category | flops | bytes accessed | tf_op | source)
XLA Modules:
  0.0 80.3 jit_solution(2933766930217039599)
XLA Ops:
  0.6 0.0 copy-start
  0.6 0.0 copy-start.1
  0.7 0.0 copy-start.2
  0.7 1.4 %load.1 = (bf16[2,32,1536]{2,1,0:T(8,128)(2,1)S(1)}, bf16[2,32,1536]{2,1,0:T(8,128)(2,1)S(1)}, bf16[2,32,1536]{2,1,0:T(8,128)(2,1)S(1)}, bf16[2,32,1536]{2,1,0:T(8,128)(2,1)S(1)}, bf16[4,128,128]{2,1,0:T(8,128)(2,1)S(1)}) custom-call(bf16[2,4,32,1536]{3,2,1,0:T(8,128)(2,1)} %bitcast.4, s32[2,128]{1,0:T(2,128)} %bitcast.5, s32[2,128]{1,0:T(2,128)} %bitcast.6, ...), custom_call_target="tpu_custom_call" | custom-call | tf_op jit(solution)/shard_map/load/pallas_call | solution.py:174
  2.1 5.5 %collective-permute-start = (bf16[2,32,1536]{2,1,0:T(8,128)(2,1)S(1)}, bf16[2,32,1536]{2,1,0:T(8,128)(2,1)S(1)}, u32[]{:S(2)}, u32[]{:S(2)}) collective-permute-start(bf16[2,32,1536]{2,1,0:T(8,128)(2,1)S(1)} %get-tuple-element.10), channel_id=1, source_target_pairs={{0,2},{1,3},{2,0},{3,1},{4,6},{5,7},{6,4},{7,5},{8,10},{9,11},{10,... | collective-permute-start | bytes 589832 | tf_op jit(solution)/shard_map/ppermute | solution.py:206
  7.6 2.8 %collective-permute-start.1 = (bf16[2,32,1536]{2,1,0:T(8,128)(2,1)S(1)}, bf16[2,32,1536]{2,1,0:T(8,128)(2,1)S(1)}, u32[]{:S(2)}, u32[]{:S(2)}) collective-permute-start(bf16[2,32,1536]{2,1,0:T(8,128)(2,1)S(1)} %get-tuple-element.11), channel_id=1, source_target_pairs={{0,1},{1,2},{2,3},{3,0},{4,7},{5,4},{6,5},{7,6},{8,9},{9,10},{10,1... | collective-permute-start | bytes 589832 | tf_op jit(solution)/shard_map/ppermute | solution.py:206
  10.4 2.5 %collective-permute-start.2 = (bf16[2,32,1536]{2,1,0:T(8,128)(2,1)S(1)}, bf16[2,32,1536]{2,1,0:T(8,128)(2,1)S(1)}, u32[]{:S(2)}, u32[]{:S(2)}) collective-permute-start(bf16[2,32,1536]{2,1,0:T(8,128)(2,1)S(1)} %get-tuple-element.12), channel_id=1, source_target_pairs={{0,3},{1,0},{2,1},{3,2},{4,5},{5,6},{6,7},{7,4},{8,11},{9,8},{10,9... | collective-permute-start | bytes 589832 | tf_op jit(solution)/shard_map/ppermute | solution.py:206
  12.9 0.0 collective-permute-done.refs_1_
  12.9 2.2 %collective-permute-done.1.refs_2_ = bf16[2,32,1536]{2,1,0:T(8,128)(2,1)S(1)} collective-permute-done((bf16[2,32,1536]{2,1,0:T(8,128)(2,1)S(1)}, bf16[2,32,1536]{2,1,0:T(8,128)(2,1)S(1)}, u32[]{:S(2)}, u32[]{:S(2)}) %collective-permute-start.1) | collective-permute-done | bytes 196640 | tf_op jit(solution)/shard_map/ppermute | solution.py:206
  15.1 6.5 %collective-permute-done.2.refs_3_ = bf16[2,32,1536]{2,1,0:T(8,128)(2,1)S(1)} collective-permute-done((bf16[2,32,1536]{2,1,0:T(8,128)(2,1)S(1)}, bf16[2,32,1536]{2,1,0:T(8,128)(2,1)S(1)}, u32[]{:S(2)}, u32[]{:S(2)}) %collective-permute-start.2) | collective-permute-done | bytes 196640 | tf_op jit(solution)/shard_map/ppermute | solution.py:206
  21.7 0.0 copy-done
  21.7 0.0 copy-done.1
  21.7 0.0 copy-done.2
  21.7 0.3 pack.1
  21.9 34.5 %all_to_all.10.pieces = bf16[128,16,128]{2,1,0:T(8,128)(2,1)S(1)} all-to-all(bf16[128,16,128]{2,1,0:T(8,128)(2,1)S(1)} %pack.1), channel_id=1, replica_groups=mesh['expert'=128,'dp'=4] {'expert'}, dimensions={0} | all-to-all | bytes 1048576 | tf_op jit(solution)/shard_map/all_to_all | solution.py:210
  56.4 0.7 update.1
  57.2 21.8 %all_to_all.11.pieces = bf16[128,5,2,128]{3,2,1,0:T(2,128)(2,1)S(1)} all-to-all(bf16[128,5,2,128]{3,2,1,0:T(2,128)(2,1)S(1)} %update.1), channel_id=1, replica_groups=mesh['expert'=128,'dp'=4] {'expert'}, dimensions={0} | all-to-all | bytes 655360 | tf_op jit(solution)/shard_map/all_to_all | solution.py:218
  78.9 1.3 %finish.1 = (f32[1,32,1536]{2,1,0:T(8,128)}, f32[1,32,1536]{2,1,0:T(8,128)}, f32[1,32,1536]{2,1,0:T(8,128)}, bf16[2,32,1536]{2,1,0:T(8,128)(2,1)}) custom-call(bf16[128,5,2,128]{3,2,1,0:T(2,128)(2,1)S(1)} %all_to_all.11.pieces, f32[1,32,1536]{2,1,0:T(8,128)S(1)} %copy-done, f32[1,32,1536]{2,1,0:T(8,128)S(1)} %copy-done.1, f32[1,32,1536]{2,1,0:T(8,128)S(1)} %copy-done.2), custom_call_target="tpu_custom_call" | custom-call | tf_op jit(solution)/shard_map/finish/pallas_call | solution.py:151
Async XLA Ops:
  0.6 21.0 %copy-start = (f32[1,32,1536]{2,1,0:T(8,128)S(1)}, f32[1,32,1536]{2,1,0:T(8,128)}, u32[]{:S(2)}) copy-start(f32[1,32,1536]{2,1,0:T(8,128)} %master.1) | copy-start | bytes 589828
  0.6 21.0 %copy-start.1 = (f32[1,32,1536]{2,1,0:T(8,128)S(1)}, f32[1,32,1536]{2,1,0:T(8,128)}, u32[]{:S(2)}) copy-start(f32[1,32,1536]{2,1,0:T(8,128)} %moment.1) | copy-start | bytes 589828
  0.7 21.0 %copy-start.2 = (f32[1,32,1536]{2,1,0:T(8,128)S(1)}, f32[1,32,1536]{2,1,0:T(8,128)}, u32[]{:S(2)}) copy-start(f32[1,32,1536]{2,1,0:T(8,128)} %second.1) | copy-start | bytes 589828
  2.1 10.8 %collective-permute-start = (bf16[2,32,1536]{2,1,0:T(8,128)(2,1)S(1)}, bf16[2,32,1536]{2,1,0:T(8,128)(2,1)S(1)}, u32[]{:S(2)}, u32[]{:S(2)}) collective-permute-start(bf16[2,32,1536]{2,1,0:T(8,128)(2,1)S(1)} %get-tuple-element.10), channel_id=1, source_target_pairs={{0,2},{1,3},{2,0},{3,1},{4,6},{5,7},{6,4},{7,5},{8,10},{9,11},{10,... | collective-permute-start | bytes 589832 | tf_op jit(solution)/shard_map/ppermute | solution.py:206
  7.6 7.6 %collective-permute-start.1 = (bf16[2,32,1536]{2,1,0:T(8,128)(2,1)S(1)}, bf16[2,32,1536]{2,1,0:T(8,128)(2,1)S(1)}, u32[]{:S(2)}, u32[]{:S(2)}) collective-permute-start(bf16[2,32,1536]{2,1,0:T(8,128)(2,1)S(1)} %get-tuple-element.11), channel_id=1, source_target_pairs={{0,1},{1,2},{2,3},{3,0},{4,7},{5,4},{6,5},{7,6},{8,9},{9,10},{10,1... | collective-permute-start | bytes 589832 | tf_op jit(solution)/shard_map/ppermute | solution.py:206
  10.4 11.3 %collective-permute-start.2 = (bf16[2,32,1536]{2,1,0:T(8,128)(2,1)S(1)}, bf16[2,32,1536]{2,1,0:T(8,128)(2,1)S(1)}, u32[]{:S(2)}, u32[]{:S(2)}) collective-permute-start(bf16[2,32,1536]{2,1,0:T(8,128)(2,1)S(1)} %get-tuple-element.12), channel_id=1, source_target_pairs={{0,3},{1,0},{2,1},{3,2},{4,5},{5,6},{6,7},{7,4},{8,11},{9,8},{10,9... | collective-permute-start | bytes 589832 | tf_op jit(solution)/shard_map/ppermute | solution.py:206

commit v6 on v5

--- a/solution.py
+++ b/solution.py
@@ -1,3 +1,5 @@
+import functools
+
 import jax
 import jax.numpy as jnp
 from jax import lax
@@ -24,9 +26,13 @@
     return new_master, new_moment, new_second
 
 
-def hot(rows, values):
+def place_of(at):
+    return ((7 - (at >> 4)) << 4) + (((4 - (at >> 1)) & 7) << 1) + (1 - (at & 1))
+
+
+def hot(rows, values, label=lambda at: at):
     at = lax.broadcasted_iota(jnp.int32, (rows, values.shape[1]), 0)
-    return (at == values).astype(jnp.bfloat16)
+    return (label(at) == values).astype(jnp.bfloat16)
 
 
 def dot(a, b, dims):
@@ -61,10 +67,13 @@
         each.wait()
     old_place, new_place, owner_slot = held_places
     _, owner_count, _ = routes.shape
-    owners = hot(owner_count, owner_slot[...])
+    owners = hot(owner_count, owner_slot[...], place_of)
+    natural = lax.broadcasted_iota(jnp.int32, (1, owner_count), 1)
+    order = hot(owner_count, natural, place_of)
     for at, place in enumerate((old_place, new_place)):
         for slot in range(slots):
             held = hot(owner_slot.shape[1], place[slot : slot + 1, :])
+            held = dot(held, order, ((1,), (1,))).astype(jnp.bfloat16)
             routes[at * slots + slot] = dot(owners, held, ((1,), (0,))).astype(routes.dtype)
     for each in grad_copies:
         each.wait()
@@ -95,7 +104,7 @@
 
 def update_kernel(pieces, routes, out, leaving):
     slots, devices = routes.shape[0] // 2, routes.shape[2]
-    lines_out = leaving.shape[0] // devices
+    lines_out = out.shape[1] * out.shape[2]
     tall = lines_out // (slots + 1)
     arrived = jnp.transpose(pieces[...], (1, 0, 2))
 
@@ -121,16 +130,16 @@
             leave(slot * tall + i, chosen[:, i * LANES : (i + 1) * LANES])
     for at in range((slots + 1) * tall, lines_out):
         leave(at, jnp.zeros((devices, LANES), jnp.float32))
-    out[...] = leaving[...].astype(out.dtype).reshape(out.shape)
+    out[...] = leaving[: devices * lines_out].astype(out.dtype).reshape(out.shape)
 
 
 def finish_kernel(pieces, master, moment, second, new_master, new_moment, new_second, replicas, arrived):
     slots, rows, cols = replicas.shape
     devices = pieces.shape[0]
-    lines = arrived.shape[0] // devices
+    lines = pieces.shape[1] * pieces.shape[2]
     quarters = devices // rows
     tall = cols // quarters // LANES
-    arrived[...] = pieces[...].reshape(arrived.shape).astype(jnp.float32)
+    arrived[: devices * lines] = pieces[...].reshape(devices * lines, LANES).astype(jnp.float32)
     for q in range(quarters):
         for i in range(tall):
             there = pl.ds((q * tall + i) * LANES, LANES)
@@ -194,6 +203,7 @@
     lines = -(-(slots + 3) * tall // 16) * 16
     pairs = -(-(slots + 1) * tall // 2)
     state = (master, moment, second)
+    message_lines = pltpu.VMEM(((devices + 8) * pairs * 2, LANES), jnp.float32)
 
     *by_rows, routes = load(grads.reshape(slots, copies, rows, cols), old_place, new_place, owner_slot)
     mine = [by_rows[0]]
@@ -207,22 +217,30 @@
     packed = call(
         pack_kernel, "pack", pltpu.VMEM((devices, lines, LANES), jnp.bfloat16), (*mine, *state)
     )
-    pieces = lax.all_to_all(packed, "expert", split_axis=0, concat_axis=0, tiled=True)
+    exchange = functools.partial(
+        lax.all_to_all,
+        axis_name="expert",
+        split_axis=0,
+        concat_axis=0,
+        tiled=True,
+        axis_index_groups=[[place_of(at) for at in range(devices)]],
+    )
+    pieces = exchange(packed)
     outbound = call(
         update_kernel,
         "update",
         pltpu.VMEM((devices, pairs, 2, LANES), jnp.bfloat16),
         (pieces, routes),
-        [pltpu.VMEM((devices * pairs * 2, LANES), jnp.float32)],
-    )
-    received = lax.all_to_all(outbound, "expert", split_axis=0, concat_axis=0, tiled=True)
+        [message_lines],
+    )
+    received = exchange(outbound)
     return call(
         finish_kernel,
         "finish",
         [jax.ShapeDtypeStruct(master.shape, jnp.float32)] * 3
         + [jax.ShapeDtypeStruct((slots, rows, cols), jnp.bfloat16)],
         (received, *state),
-        [pltpu.VMEM((devices * pairs * 2, LANES), jnp.float32)],
+        [message_lines],
     )
 
 

time: 80.6 us -> 76.3 us (0.947)
  blocking collectives: 56.3 us -> 51.8 us
    all_to_all x2, blocking collectives: 56.3 us -> 51.8 us  [the longest x1 30.4 us: on_device(): pieces = exchange(packed)]
where the time goes in v6:
time: 76.3 us; the launch traced here: 76.1 us
  blocking collectives  51.8 us (68%)
  starting transfers between devices  10.8 us (14%)
  waiting for transfers between devices  8.76 us (11%)
  Pallas kernels  4 us (5%)
    all_to_all x1, blocking collectives, on_device(): pieces = exchange(packed)  30.4 us
    all_to_all x1, blocking collectives, on_device(): received = exchange(outbound)  21.4 us
    ppermute x3, starting transfers between devices, on_device(): mine.append(lax.ppermute(by_rows[n], ('expert', 'dp'), moves))  10.8 us
    ppermute x3, waiting for transfers between devices, on_device(): mine.append(lax.ppermute(by_rows[n], ('expert', 'dp'), moves))  8.76 us
    pallas_call x3, Pallas kernels, call(): pl.pallas_call(kernel, out_shape=outs, in_specs=[in_vmem] * len(args), ou...  2.31 us
    pallas_call x1, Pallas kernels, load(): pl.pallas_call(kernel, out_shape=[*[pltpu.VMEM((slots, rows, cols), grads...  1.69 us
  transfers between devices with their start and end apart: 3, of which 2 were waited for; matrix products, arithmetic and copies ran while one was open for 0% of the time, Pallas kernels for 0%

profile of v6, /device:TPU:1, one launch (start us, length us, event | category | flops | bytes accessed | tf_op | source)
XLA Modules:
  0.0 76.1 jit_solution(5736180560777107156)
XLA Ops:
  0.6 0.0 copy-start
  0.6 0.0 copy-start.1
  0.7 0.0 copy-start.2
  0.7 1.7 %load.1 = (bf16[2,32,1536]{2,1,0:T(8,128)(2,1)S(1)}, bf16[2,32,1536]{2,1,0:T(8,128)(2,1)S(1)}, bf16[2,32,1536]{2,1,0:T(8,128)(2,1)S(1)}, bf16[2,32,1536]{2,1,0:T(8,128)(2,1)S(1)}, bf16[4,128,128]{2,1,0:T(8,128)(2,1)S(1)}) custom-call(bf16[2,4,32,1536]{3,2,1,0:T(8,128)(2,1)} %bitcast.4, s32[2,128]{1,0:T(2,128)} %bitcast.5, s32[2,128]{1,0:T(2,128)} %bitcast.6, ...), custom_call_target="tpu_custom_call" | custom-call | tf_op jit(solution)/shard_map/load/pallas_call | solution.py:183
  2.4 5.5 %collective-permute-start = (bf16[2,32,1536]{2,1,0:T(8,128)(2,1)S(1)}, bf16[2,32,1536]{2,1,0:T(8,128)(2,1)S(1)}, u32[]{:S(2)}, u32[]{:S(2)}) collective-permute-start(bf16[2,32,1536]{2,1,0:T(8,128)(2,1)S(1)} %get-tuple-element.10), channel_id=1, source_target_pairs={{0,2},{1,3},{2,0},{3,1},{4,6},{5,7},{6,4},{7,5},{8,10},{9,11},{10,... | collective-permute-start | bytes 589832 | tf_op jit(solution)/shard_map/ppermute | solution.py:216
  7.8 2.8 %collective-permute-start.1 = (bf16[2,32,1536]{2,1,0:T(8,128)(2,1)S(1)}, bf16[2,32,1536]{2,1,0:T(8,128)(2,1)S(1)}, u32[]{:S(2)}, u32[]{:S(2)}) collective-permute-start(bf16[2,32,1536]{2,1,0:T(8,128)(2,1)S(1)} %get-tuple-element.11), channel_id=1, source_target_pairs={{0,1},{1,2},{2,3},{3,0},{4,7},{5,4},{6,5},{7,6},{8,9},{9,10},{10,1... | collective-permute-start | bytes 589832 | tf_op jit(solution)/shard_map/ppermute | solution.py:216
  10.6 2.5 %collective-permute-start.2 = (bf16[2,32,1536]{2,1,0:T(8,128)(2,1)S(1)}, bf16[2,32,1536]{2,1,0:T(8,128)(2,1)S(1)}, u32[]{:S(2)}, u32[]{:S(2)}) collective-permute-start(bf16[2,32,1536]{2,1,0:T(8,128)(2,1)S(1)} %get-tuple-element.12), channel_id=1, source_target_pairs={{0,3},{1,0},{2,1},{3,2},{4,5},{5,6},{6,7},{7,4},{8,11},{9,8},{10,9... | collective-permute-start | bytes 589832 | tf_op jit(solution)/shard_map/ppermute | solution.py:216
  13.1 0.0 collective-permute-done.refs_1_
  13.2 2.2 %collective-permute-done.1.refs_2_ = bf16[2,32,1536]{2,1,0:T(8,128)(2,1)S(1)} collective-permute-done((bf16[2,32,1536]{2,1,0:T(8,128)(2,1)S(1)}, bf16[2,32,1536]{2,1,0:T(8,128)(2,1)S(1)}, u32[]{:S(2)}, u32[]{:S(2)}) %collective-permute-start.1) | collective-permute-done | bytes 196640 | tf_op jit(solution)/shard_map/ppermute | solution.py:216
  15.4 6.5 %collective-permute-done.2.refs_3_ = bf16[2,32,1536]{2,1,0:T(8,128)(2,1)S(1)} collective-permute-done((bf16[2,32,1536]{2,1,0:T(8,128)(2,1)S(1)}, bf16[2,32,1536]{2,1,0:T(8,128)(2,1)S(1)}, u32[]{:S(2)}, u32[]{:S(2)}) %collective-permute-start.2) | collective-permute-done | bytes 196640 | tf_op jit(solution)/shard_map/ppermute | solution.py:216
  21.9 0.0 copy-done
  21.9 0.0 copy-done.1
  21.9 0.0 copy-done.2
  21.9 0.3 pack.1
  22.2 30.4 %all_to_all.10.pieces = bf16[128,16,128]{2,1,0:T(8,128)(2,1)S(1)} all-to-all(bf16[128,16,128]{2,1,0:T(8,128)(2,1)S(1)} %pack.1), channel_id=1, replica_groups={{484,480,476,472,468,464,460,456,452,448,508,504,500,496,492,488,420,41..., dimensions={0} | all-to-all | bytes 1048576 | tf_op jit(solution)/shard_map/all_to_all | solution.py:228
  52.6 0.7 update.1
  53.3 21.4 %all_to_all.11.pieces = bf16[128,5,2,128]{3,2,1,0:T(2,128)(2,1)S(1)} all-to-all(bf16[128,5,2,128]{3,2,1,0:T(2,128)(2,1)S(1)} %update.1), channel_id=1, replica_groups={{484,480,476,472,468,464,460,456,452,448,508,504,500,496,492,488,420,41..., dimensions={0} | all-to-all | bytes 655360 | tf_op jit(solution)/shard_map/all_to_all | solution.py:236
  74.7 1.3 %finish.1 = (f32[1,32,1536]{2,1,0:T(8,128)}, f32[1,32,1536]{2,1,0:T(8,128)}, f32[1,32,1536]{2,1,0:T(8,128)}, bf16[2,32,1536]{2,1,0:T(8,128)(2,1)}) custom-call(bf16[128,5,2,128]{3,2,1,0:T(2,128)(2,1)S(1)} %all_to_all.11.pieces, f32[1,32,1536]{2,1,0:T(8,128)S(1)} %copy-done, f32[1,32,1536]{2,1,0:T(8,128)S(1)} %copy-done.1, f32[1,32,1536]{2,1,0:T(8,128)S(1)} %copy-done.2), custom_call_target="tpu_custom_call" | custom-call | tf_op jit(solution)/shard_map/finish/pallas_call | solution.py:160
Async XLA Ops:
  0.6 21.3 %copy-start = (f32[1,32,1536]{2,1,0:T(8,128)S(1)}, f32[1,32,1536]{2,1,0:T(8,128)}, u32[]{:S(2)}) copy-start(f32[1,32,1536]{2,1,0:T(8,128)} %master.1) | copy-start | bytes 589828
  0.6 21.3 %copy-start.1 = (f32[1,32,1536]{2,1,0:T(8,128)S(1)}, f32[1,32,1536]{2,1,0:T(8,128)}, u32[]{:S(2)}) copy-start(f32[1,32,1536]{2,1,0:T(8,128)} %moment.1) | copy-start | bytes 589828
  0.7 21.3 %copy-start.2 = (f32[1,32,1536]{2,1,0:T(8,128)S(1)}, f32[1,32,1536]{2,1,0:T(8,128)}, u32[]{:S(2)}) copy-start(f32[1,32,1536]{2,1,0:T(8,128)} %second.1) | copy-start | bytes 589828
  2.4 10.8 %collective-permute-start = (bf16[2,32,1536]{2,1,0:T(8,128)(2,1)S(1)}, bf16[2,32,1536]{2,1,0:T(8,128)(2,1)S(1)}, u32[]{:S(2)}, u32[]{:S(2)}) collective-permute-start(bf16[2,32,1536]{2,1,0:T(8,128)(2,1)S(1)} %get-tuple-element.10), channel_id=1, source_target_pairs={{0,2},{1,3},{2,0},{3,1},{4,6},{5,7},{6,4},{7,5},{8,10},{9,11},{10,... | collective-permute-start | bytes 589832 | tf_op jit(solution)/shard_map/ppermute | solution.py:216
  7.8 7.6 %collective-permute-start.1 = (bf16[2,32,1536]{2,1,0:T(8,128)(2,1)S(1)}, bf16[2,32,1536]{2,1,0:T(8,128)(2,1)S(1)}, u32[]{:S(2)}, u32[]{:S(2)}) collective-permute-start(bf16[2,32,1536]{2,1,0:T(8,128)(2,1)S(1)} %get-tuple-element.11), channel_id=1, source_target_pairs={{0,1},{1,2},{2,3},{3,0},{4,7},{5,4},{6,5},{7,6},{8,9},{9,10},{10,1... | collective-permute-start | bytes 589832 | tf_op jit(solution)/shard_map/ppermute | solution.py:216
  10.6 11.3 %collective-permute-start.2 = (bf16[2,32,1536]{2,1,0:T(8,128)(2,1)S(1)}, bf16[2,32,1536]{2,1,0:T(8,128)(2,1)S(1)}, u32[]{:S(2)}, u32[]{:S(2)}) collective-permute-start(bf16[2,32,1536]{2,1,0:T(8,128)(2,1)S(1)} %get-tuple-element.12), channel_id=1, source_target_pairs={{0,3},{1,0},{2,1},{3,2},{4,5},{5,6},{6,7},{7,4},{8,11},{9,8},{10,9... | collective-permute-start | bytes 589832 | tf_op jit(solution)/shard_map/ppermute | solution.py:216

commit v7 on v6

--- a/solution.py
+++ b/solution.py
@@ -27,7 +27,7 @@
 
 
 def place_of(at):
-    return ((7 - (at >> 4)) << 4) + (((4 - (at >> 1)) & 7) << 1) + (1 - (at & 1))
+    return (((5 - (at >> 4)) & 7) << 4) + (((4 - (at >> 1)) & 7) << 1) + (1 - (at & 1))
 
 
 def hot(rows, values, label=lambda at: at):

time: 76.3 us -> 75 us (0.983)
  blocking collectives: 51.8 us -> 50.4 us
    all_to_all x1, blocking collectives: 30.4 us -> 29.1 us  [on_device(): pieces = exchange(packed)]
where the time goes in v7:
time: 75 us; the launch traced here: 74.7 us
  blocking collectives  50.4 us (67%)
  starting transfers between devices  10.8 us (14%)
  waiting for transfers between devices  8.76 us (12%)
  Pallas kernels  4 us (5%)
    all_to_all x1, blocking collectives, on_device(): pieces = exchange(packed)  29.1 us
    all_to_all x1, blocking collectives, on_device(): received = exchange(outbound)  21.3 us
    ppermute x3, starting transfers between devices, on_device(): mine.append(lax.ppermute(by_rows[n], ('expert', 'dp'), moves))  10.8 us
    ppermute x3, waiting for transfers between devices, on_device(): mine.append(lax.ppermute(by_rows[n], ('expert', 'dp'), moves))  8.76 us
    pallas_call x3, Pallas kernels, call(): pl.pallas_call(kernel, out_shape=outs, in_specs=[in_vmem] * len(args), ou...  2.31 us
    pallas_call x1, Pallas kernels, load(): pl.pallas_call(kernel, out_shape=[*[pltpu.VMEM((slots, rows, cols), grads...  1.69 us
  transfers between devices with their start and end apart: 3, of which 2 were waited for; matrix products, arithmetic and copies ran while one was open for 0% of the time, Pallas kernels for 0%

profile of v7, /device:TPU:1, one launch (start us, length us, event | category | flops | bytes accessed | tf_op | source)
XLA Modules:
  0.0 74.7 jit_solution(10362672032978323460)
XLA Ops:
  0.6 0.0 copy-start
  0.6 0.0 copy-start.1
  0.7 0.0 copy-start.2
  0.7 1.7 %load.1 = (bf16[2,32,1536]{2,1,0:T(8,128)(2,1)S(1)}, bf16[2,32,1536]{2,1,0:T(8,128)(2,1)S(1)}, bf16[2,32,1536]{2,1,0:T(8,128)(2,1)S(1)}, bf16[2,32,1536]{2,1,0:T(8,128)(2,1)S(1)}, bf16[4,128,128]{2,1,0:T(8,128)(2,1)S(1)}) custom-call(bf16[2,4,32,1536]{3,2,1,0:T(8,128)(2,1)} %bitcast.4, s32[2,128]{1,0:T(2,128)} %bitcast.5, s32[2,128]{1,0:T(2,128)} %bitcast.6, ...), custom_call_target="tpu_custom_call" | custom-call | tf_op jit(solution)/shard_map/load/pallas_call | solution.py:183
  2.4 5.5 %collective-permute-start = (bf16[2,32,1536]{2,1,0:T(8,128)(2,1)S(1)}, bf16[2,32,1536]{2,1,0:T(8,128)(2,1)S(1)}, u32[]{:S(2)}, u32[]{:S(2)}) collective-permute-start(bf16[2,32,1536]{2,1,0:T(8,128)(2,1)S(1)} %get-tuple-element.10), channel_id=1, source_target_pairs={{0,2},{1,3},{2,0},{3,1},{4,6},{5,7},{6,4},{7,5},{8,10},{9,11},{10,... | collective-permute-start | bytes 589832 | tf_op jit(solution)/shard_map/ppermute | solution.py:216
  7.8 2.8 %collective-permute-start.1 = (bf16[2,32,1536]{2,1,0:T(8,128)(2,1)S(1)}, bf16[2,32,1536]{2,1,0:T(8,128)(2,1)S(1)}, u32[]{:S(2)}, u32[]{:S(2)}) collective-permute-start(bf16[2,32,1536]{2,1,0:T(8,128)(2,1)S(1)} %get-tuple-element.11), channel_id=1, source_target_pairs={{0,1},{1,2},{2,3},{3,0},{4,7},{5,4},{6,5},{7,6},{8,9},{9,10},{10,1... | collective-permute-start | bytes 589832 | tf_op jit(solution)/shard_map/ppermute | solution.py:216
  10.6 2.5 %collective-permute-start.2 = (bf16[2,32,1536]{2,1,0:T(8,128)(2,1)S(1)}, bf16[2,32,1536]{2,1,0:T(8,128)(2,1)S(1)}, u32[]{:S(2)}, u32[]{:S(2)}) collective-permute-start(bf16[2,32,1536]{2,1,0:T(8,128)(2,1)S(1)} %get-tuple-element.12), channel_id=1, source_target_pairs={{0,3},{1,0},{2,1},{3,2},{4,5},{5,6},{6,7},{7,4},{8,11},{9,8},{10,9... | collective-permute-start | bytes 589832 | tf_op jit(solution)/shard_map/ppermute | solution.py:216
  13.1 0.0 collective-permute-done.refs_1_
  13.2 2.2 %collective-permute-done.1.refs_2_ = bf16[2,32,1536]{2,1,0:T(8,128)(2,1)S(1)} collective-permute-done((bf16[2,32,1536]{2,1,0:T(8,128)(2,1)S(1)}, bf16[2,32,1536]{2,1,0:T(8,128)(2,1)S(1)}, u32[]{:S(2)}, u32[]{:S(2)}) %collective-permute-start.1) | collective-permute-done | bytes 196640 | tf_op jit(solution)/shard_map/ppermute | solution.py:216
  15.4 6.5 %collective-permute-done.2.refs_3_ = bf16[2,32,1536]{2,1,0:T(8,128)(2,1)S(1)} collective-permute-done((bf16[2,32,1536]{2,1,0:T(8,128)(2,1)S(1)}, bf16[2,32,1536]{2,1,0:T(8,128)(2,1)S(1)}, u32[]{:S(2)}, u32[]{:S(2)}) %collective-permute-start.2) | collective-permute-done | bytes 196640 | tf_op jit(solution)/shard_map/ppermute | solution.py:216
  21.9 0.0 copy-done
  21.9 0.0 copy-done.1
  21.9 0.0 copy-done.2
  21.9 0.3 pack.1
  22.2 29.1 %all_to_all.10.pieces = bf16[128,16,128]{2,1,0:T(8,128)(2,1)S(1)} all-to-all(bf16[128,16,128]{2,1,0:T(8,128)(2,1)S(1)} %pack.1), channel_id=1, replica_groups={{356,352,348,344,340,336,332,328,324,320,380,376,372,368,364,360,292,28..., dimensions={0} | all-to-all | bytes 1048576 | tf_op jit(solution)/shard_map/all_to_all | solution.py:228
  51.4 0.7 update.1
  52.1 21.3 %all_to_all.11.pieces = bf16[128,5,2,128]{3,2,1,0:T(2,128)(2,1)S(1)} all-to-all(bf16[128,5,2,128]{3,2,1,0:T(2,128)(2,1)S(1)} %update.1), channel_id=1, replica_groups={{356,352,348,344,340,336,332,328,324,320,380,376,372,368,364,360,292,28..., dimensions={0} | all-to-all | bytes 655360 | tf_op jit(solution)/shard_map/all_to_all | solution.py:236
  73.3 1.3 %finish.1 = (f32[1,32,1536]{2,1,0:T(8,128)}, f32[1,32,1536]{2,1,0:T(8,128)}, f32[1,32,1536]{2,1,0:T(8,128)}, bf16[2,32,1536]{2,1,0:T(8,128)(2,1)}) custom-call(bf16[128,5,2,128]{3,2,1,0:T(2,128)(2,1)S(1)} %all_to_all.11.pieces, f32[1,32,1536]{2,1,0:T(8,128)S(1)} %copy-done, f32[1,32,1536]{2,1,0:T(8,128)S(1)} %copy-done.1, f32[1,32,1536]{2,1,0:T(8,128)S(1)} %copy-done.2), custom_call_target="tpu_custom_call" | custom-call | tf_op jit(solution)/shard_map/finish/pallas_call | solution.py:160
Async XLA Ops:
  0.6 21.3 %copy-start = (f32[1,32,1536]{2,1,0:T(8,128)S(1)}, f32[1,32,1536]{2,1,0:T(8,128)}, u32[]{:S(2)}) copy-start(f32[1,32,1536]{2,1,0:T(8,128)} %master.1) | copy-start | bytes 589828
  0.6 21.3 %copy-start.1 = (f32[1,32,1536]{2,1,0:T(8,128)S(1)}, f32[1,32,1536]{2,1,0:T(8,128)}, u32[]{:S(2)}) copy-start(f32[1,32,1536]{2,1,0:T(8,128)} %moment.1) | copy-start | bytes 589828
  0.7 21.3 %copy-start.2 = (f32[1,32,1536]{2,1,0:T(8,128)S(1)}, f32[1,32,1536]{2,1,0:T(8,128)}, u32[]{:S(2)}) copy-start(f32[1,32,1536]{2,1,0:T(8,128)} %second.1) | copy-start | bytes 589828
  2.4 10.8 %collective-permute-start = (bf16[2,32,1536]{2,1,0:T(8,128)(2,1)S(1)}, bf16[2,32,1536]{2,1,0:T(8,128)(2,1)S(1)}, u32[]{:S(2)}, u32[]{:S(2)}) collective-permute-start(bf16[2,32,1536]{2,1,0:T(8,128)(2,1)S(1)} %get-tuple-element.10), channel_id=1, source_target_pairs={{0,2},{1,3},{2,0},{3,1},{4,6},{5,7},{6,4},{7,5},{8,10},{9,11},{10,... | collective-permute-start | bytes 589832 | tf_op jit(solution)/shard_map/ppermute | solution.py:216
  7.8 7.6 %collective-permute-start.1 = (bf16[2,32,1536]{2,1,0:T(8,128)(2,1)S(1)}, bf16[2,32,1536]{2,1,0:T(8,128)(2,1)S(1)}, u32[]{:S(2)}, u32[]{:S(2)}) collective-permute-start(bf16[2,32,1536]{2,1,0:T(8,128)(2,1)S(1)} %get-tuple-element.11), channel_id=1, source_target_pairs={{0,1},{1,2},{2,3},{3,0},{4,7},{5,4},{6,5},{7,6},{8,9},{9,10},{10,1... | collective-permute-start | bytes 589832 | tf_op jit(solution)/shard_map/ppermute | solution.py:216
  10.6 11.3 %collective-permute-start.2 = (bf16[2,32,1536]{2,1,0:T(8,128)(2,1)S(1)}, bf16[2,32,1536]{2,1,0:T(8,128)(2,1)S(1)}, u32[]{:S(2)}, u32[]{:S(2)}) collective-permute-start(bf16[2,32,1536]{2,1,0:T(8,128)(2,1)S(1)} %get-tuple-element.12), channel_id=1, source_target_pairs={{0,3},{1,0},{2,1},{3,2},{4,5},{5,6},{6,7},{7,4},{8,11},{9,8},{10,9... | collective-permute-start | bytes 589832 | tf_op jit(solution)/shard_map/ppermute | solution.py:216

commit v8 on v3

--- a/solution.py
+++ b/solution.py
@@ -1,3 +1,5 @@
+import functools
+
 import jax
 import jax.numpy as jnp
 from jax import lax
@@ -24,13 +26,21 @@
     return new_master, new_moment, new_second
 
 
-def hot(rows, values):
+def place_of(at):
+    return (((5 - (at >> 4)) & 7) << 4) + (((4 - (at >> 1)) & 7) << 1) + (1 - (at & 1))
+
+
+def hot(rows, values, label=lambda at: at):
     at = lax.broadcasted_iota(jnp.int32, (rows, values.shape[1]), 0)
-    return (at == values).astype(jnp.bfloat16)
+    return (label(at) == values).astype(jnp.bfloat16)
 
 
 def dot(a, b, dims):
     return lax.dot_general(a, b, (dims, ((), ())), preferred_element_type=jnp.float32)
+
+
+def dp_place_of(at, copies):
+    return (copies // 2 - at) % copies
 
 
 def load_kernel(grads, places, by_rows, routes, held_places, sems):
@@ -41,10 +51,12 @@
     ]
     grad_copies = [
         pltpu.make_async_copy(
-            grads.at[slot, copy], by_rows.at[copy, slot], sems.at[slot * copies + copy]
+            grads.at[slot, dp_place_of(at, copies)],
+            by_rows.at[at, slot],
+            sems.at[slot * copies + at],
         )
         for slot in range(slots)
-        for copy in range(copies)
+        for at in range(copies)
     ]
     for each in index_copies + grad_copies:
         each.start()
@@ -52,10 +64,13 @@
         each.wait()
     old_place, new_place, owner_slot = held_places
     _, owner_count, _ = routes.shape
-    owners = hot(owner_count, owner_slot[...])
+    owners = hot(owner_count, owner_slot[...], place_of)
+    natural = lax.broadcasted_iota(jnp.int32, (1, owner_count), 1)
+    order = hot(owner_count, natural, place_of)
     for at, place in enumerate((old_place, new_place)):
         for slot in range(slots):
             held = hot(owner_slot.shape[1], place[slot : slot + 1, :])
+            held = dot(held, order, ((1,), (1,))).astype(jnp.bfloat16)
             routes[at * slots + slot] = dot(owners, held, ((1,), (0,))).astype(routes.dtype)
     for each in grad_copies:
         each.wait()
@@ -84,7 +99,7 @@
 
 def update_kernel(pieces, routes, out, leaving):
     slots, devices = routes.shape[0] // 2, routes.shape[2]
-    lines_out = leaving.shape[0] // devices
+    lines_out = out.shape[1] * out.shape[2]
     tall = lines_out // (slots + 1)
     arrived = jnp.transpose(pieces[...], (1, 0, 2))
 
@@ -110,16 +125,16 @@
             leave(slot * tall + i, chosen[:, i * LANES : (i + 1) * LANES])
     for at in range((slots + 1) * tall, lines_out):
         leave(at, jnp.zeros((devices, LANES), jnp.float32))
-    out[...] = leaving[...].astype(out.dtype).reshape(out.shape)
+    out[...] = leaving[: devices * lines_out].astype(out.dtype).reshape(out.shape)
 
 
 def finish_kernel(pieces, master, moment, second, new_master, new_moment, new_second, replicas, arrived):
     slots, rows, cols = replicas.shape
     devices = pieces.shape[0]
-    lines = arrived.shape[0] // devices
+    lines = pieces.shape[1] * pieces.shape[2]
     quarters = devices // rows
     tall = cols // quarters // LANES
-    arrived[...] = pieces[...].reshape(arrived.shape).astype(jnp.float32)
+    arrived[: devices * lines] = pieces[...].reshape(devices * lines, LANES).astype(jnp.float32)
     for q in range(quarters):
         for i in range(tall):
             there = pl.ds((q * tall + i) * LANES, LANES)
@@ -180,28 +195,44 @@
     lines = -(-(slots + 3) * tall // 16) * 16
     pairs = -(-(slots + 1) * tall // 2)
     state = (master, moment, second)
+    message_lines = pltpu.VMEM(((devices + 8) * pairs * 2, LANES), jnp.float32)
 
     by_rows, routes = load(grads.reshape(slots, copies, rows, cols), old_place, new_place, owner_slot)
-    mine = lax.all_to_all(by_rows, "dp", split_axis=0, concat_axis=0, tiled=True)
+    mine = lax.all_to_all(
+        by_rows,
+        "dp",
+        split_axis=0,
+        concat_axis=0,
+        tiled=True,
+        axis_index_groups=[[dp_place_of(at, copies) for at in range(copies)]],
+    )
     packed = call(
         pack_kernel, "pack", pltpu.VMEM((devices, lines, LANES), jnp.bfloat16), (mine, *state)
     )
-    pieces = lax.all_to_all(packed, "expert", split_axis=0, concat_axis=0, tiled=True)
+    exchange = functools.partial(
+        lax.all_to_all,
+        axis_name="expert",
+        split_axis=0,
+        concat_axis=0,
+        tiled=True,
+        axis_index_groups=[[place_of(at) for at in range(devices)]],
+    )
+    pieces = exchange(packed)
     outbound = call(
         update_kernel,
         "update",
         pltpu.VMEM((devices, pairs, 2, LANES), jnp.bfloat16),
         (pieces, routes),
-        [pltpu.VMEM((devices * pairs * 2, LANES), jnp.float32)],
-    )
-    received = lax.all_to_all(outbound, "expert", split_axis=0, concat_axis=0, tiled=True)
+        [message_lines],
+    )
+    received = exchange(outbound)
     return call(
         finish_kernel,
         "finish",
         [jax.ShapeDtypeStruct(master.shape, jnp.float32)] * 3
         + [jax.ShapeDtypeStruct((slots, rows, cols), jnp.bfloat16)],
         (received, *state),
-        [pltpu.VMEM((devices * pairs * 2, LANES), jnp.float32)],
+        [message_lines],
     )
 
 

time: 81.7 us -> 74.8 us (0.916)
  blocking collectives: 77.1 us -> 69.9 us
    all_to_all x3, blocking collectives: 77.1 us -> 69.9 us  [the longest x1 36.9 us: on_device(): pieces = exchange(packed)]
where the time goes in v8:
time: 74.8 us; the launch traced here: 74.5 us
  blocking collectives  69.9 us (93%)
  Pallas kernels  3.94 us (5%)
    all_to_all x1, blocking collectives, on_device(): pieces = exchange(packed)  36.9 us
    all_to_all x1, blocking collectives, on_device(): received = exchange(outbound)  21.3 us
    all_to_all x1, blocking collectives, on_device(): lax.all_to_all(by_rows, 'dp', split_axis=0, concat_axis=0, tiled=True, ax...  11.8 us
    pallas_call x3, Pallas kernels, call(): pl.pallas_call(kernel, out_shape=outs, in_specs=[in_vmem] * len(args), ou...  2.31 us
    pallas_call x1, Pallas kernels, load(): pl.pallas_call(kernel, out_shape=[pltpu.VMEM((copies, slots, rows, cols),...  1.63 us

profile of v8, /device:TPU:1, one launch (start us, length us, event | category | flops | bytes accessed | tf_op | source)
XLA Modules:
  0.0 74.5 jit_solution(3648624820352660609)
XLA Ops:
  0.6 1.6 %load.1 = (bf16[4,2,32,1536]{3,2,1,0:T(8,128)(2,1)S(1)}, bf16[4,128,128]{2,1,0:T(8,128)(2,1)S(1)}) custom-call(bf16[2,4,32,1536]{3,2,1,0:T(8,128)(2,1)} %bitcast.4, s32[2,128]{1,0:T(2,128)} %bitcast.5, s32[2,128]{1,0:T(2,128)} %bitcast.6, s32[1,128]{1,0:T(1,128)} %bitcast.7), custom_call_target="tpu_custom_call" | custom-call | tf_op jit(solution)/shard_map/load/pallas_call | solution.py:175
  2.3 0.0 copy-start
  2.3 0.0 copy-start.1
  2.3 0.0 copy-start.2
  2.3 11.8 %all_to_all.15.grads = bf16[4,2,32,1536]{3,2,1,0:T(8,128)(2,1)S(1)} all-to-all(bf16[4,2,32,1536]{3,2,1,0:T(8,128)(2,1)S(1)} %get-tuple-element.6), channel_id=1, replica_groups={{2,1,0,3},{6,5,4,7},{10,9,8,11},{14,13,12,15},{18,17,16,19},{22,21,20,2..., dimensions={0} | all-to-all | bytes 1572864 | tf_op jit(solution)/shard_map/all_to_all | solution.py:201
  14.1 0.0 copy-done
  14.1 0.0 copy-done.1
  14.1 0.0 copy-done.2
  14.1 0.3 pack.1
  14.4 36.9 %all_to_all.16.pieces = bf16[128,16,128]{2,1,0:T(8,128)(2,1)S(1)} all-to-all(bf16[128,16,128]{2,1,0:T(8,128)(2,1)S(1)} %pack.1), channel_id=1, replica_groups={{356,352,348,344,340,336,332,328,324,320,380,376,372,368,364,360,292,28..., dimensions={0} | all-to-all | bytes 1048576 | tf_op jit(solution)/shard_map/all_to_all | solution.py:220
  51.2 0.7 update.1
  51.9 21.3 %all_to_all.17.pieces = bf16[128,5,2,128]{3,2,1,0:T(2,128)(2,1)S(1)} all-to-all(bf16[128,5,2,128]{3,2,1,0:T(2,128)(2,1)S(1)} %update.1), channel_id=1, replica_groups={{356,352,348,344,340,336,332,328,324,320,380,376,372,368,364,360,292,28..., dimensions={0} | all-to-all | bytes 655360 | tf_op jit(solution)/shard_map/all_to_all | solution.py:228
  73.2 1.3 %finish.1 = (f32[1,32,1536]{2,1,0:T(8,128)}, f32[1,32,1536]{2,1,0:T(8,128)}, f32[1,32,1536]{2,1,0:T(8,128)}, bf16[2,32,1536]{2,1,0:T(8,128)(2,1)}) custom-call(bf16[128,5,2,128]{3,2,1,0:T(2,128)(2,1)S(1)} %all_to_all.17.pieces, f32[1,32,1536]{2,1,0:T(8,128)S(1)} %copy-done, f32[1,32,1536]{2,1,0:T(8,128)S(1)} %copy-done.1, f32[1,32,1536]{2,1,0:T(8,128)S(1)} %copy-done.2), custom_call_target="tpu_custom_call" | custom-call | tf_op jit(solution)/shard_map/finish/pallas_call | solution.py:155
Async XLA Ops:
  2.3 11.8 %copy-start = (f32[1,32,1536]{2,1,0:T(8,128)S(1)}, f32[1,32,1536]{2,1,0:T(8,128)}, u32[]{:S(2)}) copy-start(f32[1,32,1536]{2,1,0:T(8,128)} %master.3) | copy-start | bytes 589828
  2.3 11.8 %copy-start.1 = (f32[1,32,1536]{2,1,0:T(8,128)S(1)}, f32[1,32,1536]{2,1,0:T(8,128)}, u32[]{:S(2)}) copy-start(f32[1,32,1536]{2,1,0:T(8,128)} %moment.3) | copy-start | bytes 589828
  2.3 11.8 %copy-start.2 = (f32[1,32,1536]{2,1,0:T(8,128)S(1)}, f32[1,32,1536]{2,1,0:T(8,128)}, u32[]{:S(2)}) copy-start(f32[1,32,1536]{2,1,0:T(8,128)} %second.3) | copy-start | bytes 589828

commit v9 on v8

--- a/solution.py
+++ b/solution.py
@@ -21,7 +21,8 @@
 def adamw(master, moment, second, grad):
     new_moment = beta_first * moment + (1.0 - beta_first) * grad
     new_second = beta_second * second + (1.0 - beta_second) * grad * grad
-    update = new_moment / scale_first / (jnp.sqrt(new_second / scale_second) + epsilon)
+    root = jnp.sqrt(new_second * (1.0 / scale_second))
+    update = new_moment * (1.0 / scale_first) / (root + epsilon)
     new_master = master - learn_rate * (update + weight_decay * master)
     return new_master, new_moment, new_second
 

time: 74.8 us -> 74.8 us (level)
  no operation moved by 1% of the time
where the time goes in v9:
time: 74.8 us; the launch traced here: 74.5 us
  blocking collectives  69.9 us (93%)
  Pallas kernels  3.94 us (5%)
    all_to_all x1, blocking collectives, on_device(): pieces = exchange(packed)  36.9 us
    all_to_all x1, blocking collectives, on_device(): received = exchange(outbound)  21.3 us
    all_to_all x1, blocking collectives, on_device(): lax.all_to_all(by_rows, 'dp', split_axis=0, concat_axis=0, tiled=True, ax...  11.8 us
    pallas_call x3, Pallas kernels, call(): pl.pallas_call(kernel, out_shape=outs, in_specs=[in_vmem] * len(args), ou...  2.31 us
    pallas_call x1, Pallas kernels, load(): pl.pallas_call(kernel, out_shape=[pltpu.VMEM((copies, slots, rows, cols),...  1.63 us

profile of v9, /device:TPU:1, one launch (start us, length us, event | category | flops | bytes accessed | tf_op | source)
XLA Modules:
  0.0 74.5 jit_solution(16173790465754474510)
XLA Ops:
  0.6 1.6 %load.1 = (bf16[4,2,32,1536]{3,2,1,0:T(8,128)(2,1)S(1)}, bf16[4,128,128]{2,1,0:T(8,128)(2,1)S(1)}) custom-call(bf16[2,4,32,1536]{3,2,1,0:T(8,128)(2,1)} %bitcast.4, s32[2,128]{1,0:T(2,128)} %bitcast.5, s32[2,128]{1,0:T(2,128)} %bitcast.6, s32[1,128]{1,0:T(1,128)} %bitcast.7), custom_call_target="tpu_custom_call" | custom-call | tf_op jit(solution)/shard_map/load/pallas_call | solution.py:176
  2.3 0.0 copy-start
  2.3 0.0 copy-start.1
  2.3 0.0 copy-start.2
  2.3 11.8 %all_to_all.15.grads = bf16[4,2,32,1536]{3,2,1,0:T(8,128)(2,1)S(1)} all-to-all(bf16[4,2,32,1536]{3,2,1,0:T(8,128)(2,1)S(1)} %get-tuple-element.6), channel_id=1, replica_groups={{2,1,0,3},{6,5,4,7},{10,9,8,11},{14,13,12,15},{18,17,16,19},{22,21,20,2..., dimensions={0} | all-to-all | bytes 1572864 | tf_op jit(solution)/shard_map/all_to_all | solution.py:202
  14.1 0.0 copy-done
  14.1 0.0 copy-done.1
  14.1 0.0 copy-done.2
  14.1 0.3 pack.1
  14.4 36.9 %all_to_all.16.pieces = bf16[128,16,128]{2,1,0:T(8,128)(2,1)S(1)} all-to-all(bf16[128,16,128]{2,1,0:T(8,128)(2,1)S(1)} %pack.1), channel_id=1, replica_groups={{356,352,348,344,340,336,332,328,324,320,380,376,372,368,364,360,292,28..., dimensions={0} | all-to-all | bytes 1048576 | tf_op jit(solution)/shard_map/all_to_all | solution.py:221
  51.2 0.7 update.1
  51.9 21.3 %all_to_all.17.pieces = bf16[128,5,2,128]{3,2,1,0:T(2,128)(2,1)S(1)} all-to-all(bf16[128,5,2,128]{3,2,1,0:T(2,128)(2,1)S(1)} %update.1), channel_id=1, replica_groups={{356,352,348,344,340,336,332,328,324,320,380,376,372,368,364,360,292,28..., dimensions={0} | all-to-all | bytes 655360 | tf_op jit(solution)/shard_map/all_to_all | solution.py:229
  73.2 1.3 %finish.1 = (f32[1,32,1536]{2,1,0:T(8,128)}, f32[1,32,1536]{2,1,0:T(8,128)}, f32[1,32,1536]{2,1,0:T(8,128)}, bf16[2,32,1536]{2,1,0:T(8,128)(2,1)}) custom-call(bf16[128,5,2,128]{3,2,1,0:T(2,128)(2,1)S(1)} %all_to_all.17.pieces, f32[1,32,1536]{2,1,0:T(8,128)S(1)} %copy-done, f32[1,32,1536]{2,1,0:T(8,128)S(1)} %copy-done.1, f32[1,32,1536]{2,1,0:T(8,128)S(1)} %copy-done.2), custom_call_target="tpu_custom_call" | custom-call | tf_op jit(solution)/shard_map/finish/pallas_call | solution.py:156
Async XLA Ops:
  2.3 11.8 %copy-start = (f32[1,32,1536]{2,1,0:T(8,128)S(1)}, f32[1,32,1536]{2,1,0:T(8,128)}, u32[]{:S(2)}) copy-start(f32[1,32,1536]{2,1,0:T(8,128)} %master.3) | copy-start | bytes 589828
  2.3 11.8 %copy-start.1 = (f32[1,32,1536]{2,1,0:T(8,128)S(1)}, f32[1,32,1536]{2,1,0:T(8,128)}, u32[]{:S(2)}) copy-start(f32[1,32,1536]{2,1,0:T(8,128)} %moment.3) | copy-start | bytes 589828
  2.3 11.8 %copy-start.2 = (f32[1,32,1536]{2,1,0:T(8,128)S(1)}, f32[1,32,1536]{2,1,0:T(8,128)}, u32[]{:S(2)}) copy-start(f32[1,32,1536]{2,1,0:T(8,128)} %second.3) | copy-start | bytes 589828
